TPU v7x, 128 devices: a whole 4x4x4 slice. The times are simulated.
128 devices in a mesh: ctx: 8 (over y, core), tp: 16 (over x, z).
Axes of the slice: x: 4, y: 4, z: 4, core: 2. Of those that a mesh axis runs over, the one named last changes fastest.
Arguments:
- tokens: bfloat16 [4096, 5120], P(('ctx', 'tp')), may hold values from -6 to 6
- grad_out: bfloat16 [4096, 5120], P(('ctx', 'tp')), may hold values from -2 to 2
- gate_prob: bfloat16 [4096], P(('ctx', 'tp')), may hold values from 0.19921875 to 1
- expert_ids: int32 [4096, 1], P(('ctx', 'tp')), may hold values from 0 to 7; in each aligned block of 32 rows (0 to 31, 32 to 63, ...) at most 6 rows name the same one
- w_gate: bfloat16 [8, 5120, 6144], P('ctx', None, 'tp'), may hold values from -0.078125 to 0.078125
- w_up: bfloat16 [8, 5120, 6144], P('ctx', None, 'tp'), may hold values from -0.078125 to 0.078125
- w_down: bfloat16 [8, 6144, 5120], P('ctx', 'tp'), may hold values from -0.078125 to 0.078125
Outputs:
- grad_tokens: bfloat16 [4096, 5120], P(('ctx', 'tp'))
- grad_prob: bfloat16 [4096], P(('ctx', 'tp'))
- grad_gate: bfloat16 [8, 5120, 6144], P('ctx', None, 'tp')
- grad_up: bfloat16 [8, 5120, 6144], P('ctx', None, 'tp')
- grad_down: bfloat16 [8, 6144, 5120], P('ctx', 'tp')
Inputs may be any that keep to these rules, and one draw needn't show every extreme that they name: `expert_ids`: among the 32 tokens of one device no expert is chosen by more than 6 tokens, and some expert is chosen by exactly 6; every expert is chosen somewhere.
All inputs are finite; a program needn't handle non-finite values.
Results may differ from a plain program's by a relative error of at most 0.0055.
Values may be sent and summed in bfloat16 or wider, within the bound.
A program may use at most 192 MiB of HBM per device.

v0:
```python
import jax
import jax.numpy as jnp
from jax import lax
from jax.sharding import PartitionSpec as P


def dispatch_table(chosen, owners, capacity):
    onehot = (chosen[:, None] == jnp.arange(owners, dtype=jnp.int32)[None, :]).astype(jnp.int32)
    slots = jnp.sum((jnp.cumsum(onehot, axis=0) - 1) * onehot, axis=1)
    target = chosen * capacity + slots
    return (jnp.arange(owners * capacity, dtype=jnp.int32)[:, None] == target[None, :]).astype(
        jnp.bfloat16
    )


def expert_grads(rows_in, rows_grad, prob, wg, wu, wd):
    g = jnp.dot(rows_in, wg, preferred_element_type=jnp.float32)
    u = jnp.dot(rows_in, wu, preferred_element_type=jnp.float32)
    sig = jax.nn.sigmoid(g)
    act = g * sig
    hidden = act * u
    probs = prob.astype(jnp.float32)[:, None]
    weighted = (probs * hidden).astype(jnp.bfloat16)
    dh_raw = lax.dot_general(
        rows_grad, wd, (((1,), (1,)), ((), ())), preferred_element_type=jnp.float32
    )
    prob_part = jnp.sum(hidden * dh_raw, axis=1)
    dh = probs * dh_raw
    dg = (dh * u * sig * (1.0 + g * (1.0 - sig))).astype(jnp.bfloat16)
    du = (dh * act).astype(jnp.bfloat16)
    grad_wd = lax.dot_general(
        weighted, rows_grad, (((0,), (0,)), ((), ())), preferred_element_type=jnp.float32
    ).astype(jnp.bfloat16)
    grad_wg = lax.dot_general(
        rows_in, dg, (((0,), (0,)), ((), ())), preferred_element_type=jnp.float32
    ).astype(jnp.bfloat16)
    grad_wu = lax.dot_general(
        rows_in, du, (((0,), (0,)), ((), ())), preferred_element_type=jnp.float32
    ).astype(jnp.bfloat16)
    input_part = lax.dot_general(
        dg, wg, (((1,), (1,)), ((), ())), preferred_element_type=jnp.float32
    )
    input_part = input_part + lax.dot_general(
        du, wu, (((1,), (1,)), ((), ())), preferred_element_type=jnp.float32
    )
    return (grad_wg, grad_wu, grad_wd, input_part, prob_part)


def per_device(tokens, grad_out, gate_prob, expert_ids, w_gate, w_up, w_down):
    owners = lax.axis_size("ctx")
    groups = lax.axis_size("tp")
    count = tokens.shape[0]
    width = tokens.shape[1]
    capacity = 3 * count // (2 * owners)
    table = dispatch_table(expert_ids[:, 0], owners, capacity)
    send_in = (
        jnp.dot(table, tokens, preferred_element_type=jnp.float32)
        .astype(jnp.bfloat16)
        .reshape(owners, capacity, width)
    )
    send_grad = (
        jnp.dot(table, grad_out, preferred_element_type=jnp.float32)
        .astype(jnp.bfloat16)
        .reshape(owners, capacity, width)
    )
    send_prob = (
        jnp.dot(table, gate_prob[:, None], preferred_element_type=jnp.float32)
        .astype(jnp.bfloat16)
        .reshape(owners, capacity)
    )
    wide_in = jnp.broadcast_to(send_in[:, None], (owners, groups, capacity, width)).reshape(
        owners * groups, capacity, width
    )
    wide_grad = jnp.broadcast_to(send_grad[:, None], (owners, groups, capacity, width)).reshape(
        owners * groups, capacity, width
    )
    wide_prob = jnp.broadcast_to(send_prob[:, None], (owners, groups, capacity)).reshape(
        owners * groups, capacity
    )
    got_in, got_grad, got_prob = (
        lax.all_to_all(wide_in, ("ctx", "tp"), split_axis=0, concat_axis=0, tiled=True),
        lax.all_to_all(wide_grad, ("ctx", "tp"), split_axis=0, concat_axis=0, tiled=True),
        lax.all_to_all(wide_prob, ("ctx", "tp"), split_axis=0, concat_axis=0, tiled=True),
    )
    grad_wg, grad_wu, grad_wd, input_part, prob_part = expert_grads(
        got_in.reshape(-1, width),
        got_grad.reshape(-1, width),
        got_prob.reshape(-1),
        w_gate[0],
        w_up[0],
        w_down[0],
    )
    back_in, back_prob = (
        lax.all_to_all(
            input_part.reshape(owners * groups, capacity, width),
            ("ctx", "tp"),
            split_axis=0,
            concat_axis=0,
            tiled=True,
        ),
        lax.all_to_all(
            prob_part.reshape(owners * groups, capacity),
            ("ctx", "tp"),
            split_axis=0,
            concat_axis=0,
            tiled=True,
        ),
    )
    final_in = jnp.sum(back_in.reshape(owners, groups, capacity, width), axis=1).astype(
        jnp.bfloat16
    )
    final_prob = jnp.sum(back_prob.reshape(owners, groups, capacity), axis=1).astype(jnp.bfloat16)
    grad_tokens = lax.dot_general(
        table,
        final_in.reshape(-1, width),
        (((0,), (0,)), ((), ())),
        preferred_element_type=jnp.float32,
    ).astype(jnp.bfloat16)
    grad_prob = lax.dot_general(
        table,
        final_prob.reshape(-1, 1),
        (((0,), (0,)), ((), ())),
        preferred_element_type=jnp.float32,
    )[:, 0].astype(jnp.bfloat16)
    return (grad_tokens, grad_prob, grad_wg[None], grad_wu[None], grad_wd[None])


def solution(mesh):
    in_specs = (
        P(("ctx", "tp"), None),
        P(("ctx", "tp"), None),
        P(("ctx", "tp")),
        P(("ctx", "tp"), None),
        P("ctx", None, "tp"),
        P("ctx", None, "tp"),
        P("ctx", "tp", None),
    )
    out_specs = (
        P(("ctx", "tp"), None),
        P(("ctx", "tp")),
        P("ctx", None, "tp"),
        P("ctx", None, "tp"),
        P("ctx", "tp", None),
    )
    return jax.shard_map(
        per_device, mesh=mesh, in_specs=in_specs, out_specs=out_specs, check_vma=False
    )
```

profile of v0, /device:TPU:0, one launch (start us, length us, event | category | flops | bytes accessed | tf_op | source)
XLA Modules:
  0.0 705.6 jit_solution(7347180438804965234)
XLA Ops:
  0.6 0.8 fusion.17
  1.5 0.8 select_reduce_fusion
  2.3 0.7 multiply_add_fusion
  3.0 0.8 fusion.13
  4.1 0.8 copy.14
  4.9 11.1 %all-to-all-start = ((bf16[128,1,6]{2,1,0:T(2,128)(2,1)}), bf16[128,1,6]{2,1,0:T(2,128)(2,1)S(1)}, u32[]{:S(2)}, u32[]{:S(2)}) async-start(bf16[128,1,6]{2,1,0:T(2,128)(2,1)} %copy.14), calls=%async_computation | async-start | bytes 131072 | tf_op jit(solution)/shard_map/all_to_all | solution.py:83
  16.1 0.3 convolution_convert_fusion.3
  16.5 8.9 %all-to-all-done = bf16[128,1,6]{2,1,0:T(2,128)(2,1)S(1)} async-done(((bf16[128,1,6]{2,1,0:T(2,128)(2,1)}), bf16[128,1,6]{2,1,0:T(2,128)(2,1)S(1)}, u32[]{:S(2)}, u32[]{:S(2)}) %all-to-all-start) | async-done | bytes 1568 | tf_op jit(solution)/shard_map/all_to_all | solution.py:83
  25.5 5.3 broadcast_in_dim.40
  30.8 6.0 all-to-all-start.2
  37.3 129.8 %all-to-all-done.2 = bf16[128,6,5120]{2,1,0:T(8,128)(2,1)} async-done(((bf16[128,6,5120]{2,1,0:T(8,128)(2,1)}), bf16[128,6,5120]{2,1,0:T(8,128)(2,1)}, u32[]{:S(2)}, u32[]{:S(2)}) %all-to-all-start.2) | async-done | bytes 7864352 | tf_op jit(solution)/shard_map/all_to_all | solution.py:81
  167.1 5.3 broadcast_in_dim.38
  172.3 11.0 %all-to-all-start.1 = ((bf16[128,6,5120]{2,1,0:T(8,128)(2,1)}), bf16[128,6,5120]{2,1,0:T(8,128)(2,1)}, u32[]{:S(2)}, u32[]{:S(2)}) async-start(bf16[128,6,5120]{2,1,0:T(8,128)(2,1)} %bitcast.58), calls=%async_computation.1 | async-start | bytes 20971520 | tf_op jit(solution)/shard_map/all_to_all | solution.py:82
  183.7 13.2 %reshape.78 = bf16[768,5120]{1,0:T(8,128)(2,1)} reshape(bf16[128,6,5120]{2,1,0:T(8,128)(2,1)} %all-to-all-done.2) | data formatting | bytes 15728640 | tf_op jit(solution)/shard_map/reshape | solution.py:86
  196.9 7.8 %fusion.5 = f32[768,384]{0,1:T(8,128)S(1)} fusion(bf16[768,5120]{1,0:T(8,128)(2,1)} %reshape.78, bf16[1,5120,384]{2,1,0:T(8,128)(2,1)} %param.11), kind=kOutput, calls=%fused_computation.13 | convolution fusion | flops 3019898880 | bytes 12976128 | tf_op jit(solution)/shard_map/dot_general | solution.py:17
  204.8 4.6 fusion.8
  209.3 102.4 %all-to-all-done.1 = bf16[128,6,5120]{2,1,0:T(8,128)(2,1)} async-done(((bf16[128,6,5120]{2,1,0:T(8,128)(2,1)}), bf16[128,6,5120]{2,1,0:T(8,128)(2,1)}, u32[]{:S(2)}, u32[]{:S(2)}) %all-to-all-start.1) | async-done | bytes 7864352 | tf_op jit(solution)/shard_map/all_to_all | solution.py:82
  311.7 13.2 %reshape.76 = bf16[768,5120]{1,0:T(8,128)(2,1)} reshape(bf16[128,6,5120]{2,1,0:T(8,128)(2,1)} %all-to-all-done.1) | data formatting | bytes 15728640 | tf_op jit(solution)/shard_map/reshape | solution.py:87
  325.0 8.4 %multiply_reduce_fusion = (f32[768]{0:T(1024)S(1)}, bf16[768,384]{0,1:T(8,128)(2,1)S(1)}, bf16[768,384]{0,1:T(8,128)(2,1)S(1)}) fusion(f32[768,384]{0,1:T(8,128)} %fusion.8, f32[768,384]{0,1:T(8,128)S(1)} %fusion.5, f32[768]{0:T(1024)S(1)} %reshape.82, bf16[768,5120]{1,0:T(8,128)(2,1)} %reshape.76, bf16[1,384,5120]{2,1,0:T(8,128)(2,1)} %param.13), kind=kOutput, calls=%fused_computation.21 | convolution fusion | flops 3024911616 | bytes 15341568 | tf_op jit(solution)/shard_map/dot_general | solution.py:24
  333.4 0.8 all_to_all.26
  334.2 11.5 %all-to-all-start.4 = ((f32[128,1,6]{2,1,0:T(1,128)}), f32[128,1,6]{2,1,0:T(1,128)S(1)}, u32[]{:S(2)}, u32[]{:S(2)}) async-start(f32[128,1,6]{2,1,0:T(1,128)} %bitcast.9), calls=%async_computation.4 | async-start | bytes 131072 | tf_op jit(solution)/shard_map/all_to_all | solution.py:101
  345.7 10.0 %fusion.3 = f32[768,5120]{1,0:T(8,128)} fusion(bf16[768,384]{0,1:T(8,128)(2,1)S(1)} %get-tuple-element.6, bf16[1,5120,384]{2,1,0:T(8,128)(2,1)} %param.11), kind=kOutput, calls=%fused_computation.11 | convolution fusion | flops 3019898880 | bytes 20250624 | tf_op jit(solution)/shard_map/dot_general | solution.py:40
  355.7 11.0 %convolution_add_fusion = f32[768,5120]{1,0:T(8,128)} fusion(f32[768,5120]{1,0:T(8,128)} %fusion.3, bf16[768,384]{0,1:T(8,128)(2,1)S(1)} %get-tuple-element.7, bf16[1,5120,384]{2,1,0:T(8,128)(2,1)S(1)} %copy-done.4), kind=kOutput, calls=%fused_computation.1 | convolution fusion | flops 3023831040 | bytes 35979264 | tf_op jit(solution)/shard_map/dot_general | solution.py:43
  366.7 17.7 %reshape.79 = f32[128,6,5120]{2,1,0:T(8,128)} reshape(f32[768,5120]{1,0:T(8,128)} %convolution_add_fusion) | data formatting | bytes 31457280 | tf_op jit(solution)/shard_map/reshape | solution.py:95
  384.4 10.0 %all-to-all-start.3 = ((f32[128,6,5120]{2,1,0:T(8,128)}), f32[128,6,5120]{2,1,0:T(8,128)}, u32[]{:S(2)}, u32[]{:S(2)}) async-start(f32[128,6,5120]{2,1,0:T(8,128)} %reshape.79), calls=%async_computation.3 | async-start | bytes 41943040 | tf_op jit(solution)/shard_map/all_to_all | solution.py:94
  394.5 9.6 %fusion = bf16[1,5120,384]{2,1,0:T(8,128)(2,1)} fusion(bf16[768,5120]{1,0:T(8,128)(2,1)} %reshape.78, bf16[768,384]{0,1:T(8,128)(2,1)S(1)} %get-tuple-element.6), kind=kOutput, calls=%fused_computation.5 | convolution fusion | flops 3021864960 | bytes 12386304 | tf_op jit(solution)/shard_map/dot_general | solution.py:34
  404.1 9.6 %fusion.1 = bf16[1,5120,384]{2,1,0:T(8,128)(2,1)} fusion(bf16[768,5120]{1,0:T(8,128)(2,1)} %reshape.78, bf16[768,384]{0,1:T(8,128)(2,1)S(1)} %get-tuple-element.7), kind=kOutput, calls=%fused_computation.6 | convolution fusion | flops 3021864960 | bytes 12386304 | tf_op jit(solution)/shard_map/dot_general | solution.py:37
  413.7 4.9 fusion.2
  418.8 0.6 fusion.14
  419.4 276.8 %all-to-all-done.3 = f32[128,6,5120]{2,1,0:T(8,128)} async-done(((f32[128,6,5120]{2,1,0:T(8,128)}), f32[128,6,5120]{2,1,0:T(8,128)}, u32[]{:S(2)}, u32[]{:S(2)}) %all-to-all-start.3) | async-done | bytes 15728672 | tf_op jit(solution)/shard_map/all_to_all | solution.py:94
  696.3 8.1 %bitcast_reduce_fusion = bf16[8,6,5120]{2,1,0:T(8,128)(2,1)S(1)} fusion(f32[128,6,5120]{2,1,0:T(8,128)} %all-to-all-done.3), kind=kLoop, calls=%fused_computation | loop fusion | flops 3686400 | bytes 16220160 | tf_op jit(solution)/shard_map/reduce_sum | solution.py:109
  704.6 1.0 convolution_convert_fusion.5
  (33 shorter events, 1.7 us)
Async XLA Ops:
  0.6 15.4 %copy-start = (bf16[32,5120]{1,0:T(8,128)(2,1)S(1)}, bf16[32,5120]{1,0:T(8,128)(2,1)}, u32[]{:S(2)}) copy-start(bf16[32,5120]{1,0:T(8,128)(2,1)} %param.7) | copy-start | bytes 983044
  4.9 20.6 %all-to-all-start = ((bf16[128,1,6]{2,1,0:T(2,128)(2,1)}), bf16[128,1,6]{2,1,0:T(2,128)(2,1)S(1)}, u32[]{:S(2)}, u32[]{:S(2)}) async-start(bf16[128,1,6]{2,1,0:T(2,128)(2,1)} %copy.14), calls=%async_computation | async-start | bytes 131072 | tf_op jit(solution)/shard_map/all_to_all | solution.py:83
  30.8 6.1 copy-start.5
  30.8 136.3 %all-to-all-start.2 = ((bf16[128,6,5120]{2,1,0:T(8,128)(2,1)}), bf16[128,6,5120]{2,1,0:T(8,128)(2,1)}, u32[]{:S(2)}, u32[]{:S(2)}) async-start(bf16[128,6,5120]{2,1,0:T(8,128)(2,1)} %bitcast.59), calls=%async_computation.2 | async-start | bytes 20971520 | tf_op jit(solution)/shard_map/all_to_all | solution.py:81
  172.3 139.4 %all-to-all-start.1 = ((bf16[128,6,5120]{2,1,0:T(8,128)(2,1)}), bf16[128,6,5120]{2,1,0:T(8,128)(2,1)}, u32[]{:S(2)}, u32[]{:S(2)}) async-start(bf16[128,6,5120]{2,1,0:T(8,128)(2,1)} %bitcast.58), calls=%async_computation.1 | async-start | bytes 20971520 | tf_op jit(solution)/shard_map/all_to_all | solution.py:82
  196.9 7.8 %copy-start.2 = (bf16[768,5120]{1,0:T(8,128)(2,1)S(1)}, bf16[768,5120]{1,0:T(8,128)(2,1)}, u32[]{:S(2)}) copy-start(bf16[768,5120]{1,0:T(8,128)(2,1)} %reshape.78) | copy-start | bytes 23592964
  196.9 7.8 %copy-start.3 = (bf16[1,5120,384]{2,1,0:T(8,128)(2,1)S(1)}, bf16[1,5120,384]{2,1,0:T(8,128)(2,1)}, u32[]{:S(2)}) copy-start(bf16[1,5120,384]{2,1,0:T(8,128)(2,1)} %param.12) | copy-start | bytes 11796484
  334.2 50.3 %all-to-all-start.4 = ((f32[128,1,6]{2,1,0:T(1,128)}), f32[128,1,6]{2,1,0:T(1,128)S(1)}, u32[]{:S(2)}, u32[]{:S(2)}) async-start(f32[128,1,6]{2,1,0:T(1,128)} %bitcast.9), calls=%async_computation.4 | async-start | bytes 131072 | tf_op jit(solution)/shard_map/all_to_all | solution.py:101
  345.7 10.0 %copy-start.4 = (bf16[1,5120,384]{2,1,0:T(8,128)(2,1)S(1)}, bf16[1,5120,384]{2,1,0:T(8,128)(2,1)}, u32[]{:S(2)}) copy-start(bf16[1,5120,384]{2,1,0:T(8,128)(2,1)} %param.12) | copy-start | bytes 11796484
  384.4 311.8 %all-to-all-start.3 = ((f32[128,6,5120]{2,1,0:T(8,128)}), f32[128,6,5120]{2,1,0:T(8,128)}, u32[]{:S(2)}, u32[]{:S(2)}) async-start(f32[128,6,5120]{2,1,0:T(8,128)} %reshape.79), calls=%async_computation.3 | async-start | bytes 41943040 | tf_op jit(solution)/shard_map/all_to_all | solution.py:94
  394.5 19.2 %slice-start = ((s8[7864320]{0:T(1024)(128)(4,1)}), s8[4194304]{0:T(1024)(128)(4,1)S(1)}, s32[]{:S(2)}) async-start(s8[7864320]{0:T(1024)(128)(4,1)} %bitcast.60), calls=%async_computation.5 | async-start | bytes 8388608
  404.1 9.6 %slice-start.1 = ((s8[7864320]{0:T(1024)(128)(4,1)}), s8[3670016]{0:T(1024)(128)(4,1)S(1)}, s32[]{:S(2)}) async-start(s8[7864320]{0:T(1024)(128)(4,1)} %bitcast.60), calls=%async_computation.6 | async-start | bytes 7340032
  404.1 9.6 %copy-start.6 = (f32[768,384]{0,1:T(8,128)S(1)}, f32[768,384]{0,1:T(8,128)}, u32[]{:S(2)}) copy-start(f32[768,384]{0,1:T(8,128)} %fusion.8) | copy-start | bytes 3538948
  696.3 9.3 %copy-start.1 = (bf16[32,5120]{1,0:T(8,128)(2,1)S(1)}, bf16[32,5120]{1,0:T(8,128)(2,1)}, u32[]{:S(2)}) copy-start(bf16[32,5120]{1,0:T(8,128)(2,1)} %param.7) | copy-start | bytes 983044
where the time goes:
time: 716 us; the launch traced here: 706 us
  waiting for transfers between devices  518 us (72%)
  matrix products  68.9 us (10%)
  local copies, waits for them, and re-layouts  57.4 us (8%)
  starting transfers between devices  49.8 us (7%)
  other arithmetic  10.7 us (1%)
    all_to_all x1, waiting for transfers between devices, per_device(): lax.all_to_all(input_part.reshape(owners * groups, capacity, width), ('ct...  277 us
    all_to_all x1, waiting for transfers between devices, per_device(): lax.all_to_all(wide_in, ('ctx', 'tp'), split_axis=0, concat_axis=0, tiled...  130 us
    all_to_all x1, waiting for transfers between devices, per_device(): lax.all_to_all(wide_grad, ('ctx', 'tp'), split_axis=0, concat_axis=0, til...  102 us
    reshape x1, local copies, waits for them, and re-layouts, per_device(): input_part.reshape(owners * groups, capacity, width)  17.7 us
  transfers between devices with their start and end apart: 5, of which 4 were waited for; matrix products, arithmetic and copies ran while one was open for 13% of the time, Pallas kernels for 0%

commit v1 on v0

--- a/solution.py
+++ b/solution.py
@@ -52,73 +52,47 @@
     count = tokens.shape[0]
     width = tokens.shape[1]
     capacity = 3 * count // (2 * owners)
+    rows = owners * capacity
     table = dispatch_table(expert_ids[:, 0], owners, capacity)
-    send_in = (
-        jnp.dot(table, tokens, preferred_element_type=jnp.float32)
-        .astype(jnp.bfloat16)
-        .reshape(owners, capacity, width)
+
+    def route(values):
+        return jnp.dot(table, values, preferred_element_type=jnp.float32).astype(jnp.bfloat16)
+
+    send = jnp.concatenate(
+        [route(tokens), route(grad_out), route(jnp.broadcast_to(gate_prob[:, None], (count, 128)))],
+        axis=1,
     )
-    send_grad = (
-        jnp.dot(table, grad_out, preferred_element_type=jnp.float32)
-        .astype(jnp.bfloat16)
-        .reshape(owners, capacity, width)
-    )
-    send_prob = (
-        jnp.dot(table, gate_prob[:, None], preferred_element_type=jnp.float32)
-        .astype(jnp.bfloat16)
-        .reshape(owners, capacity)
-    )
-    wide_in = jnp.broadcast_to(send_in[:, None], (owners, groups, capacity, width)).reshape(
-        owners * groups, capacity, width
-    )
-    wide_grad = jnp.broadcast_to(send_grad[:, None], (owners, groups, capacity, width)).reshape(
-        owners * groups, capacity, width
-    )
-    wide_prob = jnp.broadcast_to(send_prob[:, None], (owners, groups, capacity)).reshape(
-        owners * groups, capacity
-    )
-    got_in, got_grad, got_prob = (
-        lax.all_to_all(wide_in, ("ctx", "tp"), split_axis=0, concat_axis=0, tiled=True),
-        lax.all_to_all(wide_grad, ("ctx", "tp"), split_axis=0, concat_axis=0, tiled=True),
-        lax.all_to_all(wide_prob, ("ctx", "tp"), split_axis=0, concat_axis=0, tiled=True),
-    )
+    plane = lax.all_to_all(
+        send.reshape(owners, capacity, -1), "ctx", split_axis=0, concat_axis=0, tiled=True
+    ).reshape(rows, -1)
+    got = lax.all_gather(plane, "tp", axis=0, tiled=True)
     grad_wg, grad_wu, grad_wd, input_part, prob_part = expert_grads(
-        got_in.reshape(-1, width),
-        got_grad.reshape(-1, width),
-        got_prob.reshape(-1),
+        got[:, :width],
+        got[:, width : 2 * width],
+        got[:, 2 * width],
         w_gate[0],
         w_up[0],
         w_down[0],
     )
-    back_in, back_prob = (
-        lax.all_to_all(
-            input_part.reshape(owners * groups, capacity, width),
-            ("ctx", "tp"),
-            split_axis=0,
-            concat_axis=0,
-            tiled=True,
-        ),
-        lax.all_to_all(
-            prob_part.reshape(owners * groups, capacity),
-            ("ctx", "tp"),
-            split_axis=0,
-            concat_axis=0,
-            tiled=True,
-        ),
+    back_in = lax.psum_scatter(
+        input_part.astype(jnp.bfloat16), "tp", scatter_dimension=0, tiled=True
     )
-    final_in = jnp.sum(back_in.reshape(owners, groups, capacity, width), axis=1).astype(
-        jnp.bfloat16
+    back_prob = lax.psum_scatter(prob_part, "tp", scatter_dimension=0, tiled=True)
+    final_in = lax.all_to_all(
+        back_in.reshape(owners, capacity, width), "ctx", split_axis=0, concat_axis=0, tiled=True
     )
-    final_prob = jnp.sum(back_prob.reshape(owners, groups, capacity), axis=1).astype(jnp.bfloat16)
+    final_prob = lax.all_to_all(
+        back_prob.reshape(owners, capacity), "ctx", split_axis=0, concat_axis=0, tiled=True
+    ).astype(jnp.bfloat16)
     grad_tokens = lax.dot_general(
         table,
-        final_in.reshape(-1, width),
+        final_in.reshape(rows, width),
         (((0,), (0,)), ((), ())),
         preferred_element_type=jnp.float32,
     ).astype(jnp.bfloat16)
     grad_prob = lax.dot_general(
         table,
-        final_prob.reshape(-1, 1),
+        final_prob.reshape(rows, 1),
         (((0,), (0,)), ((), ())),
         preferred_element_type=jnp.float32,
     )[:, 0].astype(jnp.bfloat16)

time: 716 us -> 297 us (0.41); the launches traced: 706 us -> 296 us
  waiting for transfers between devices: 518 us -> 129 us
  blocking collectives: 0 us -> 62.4 us
  local copies, waits for them, and re-layouts: 57.4 us -> 5.35 us
  starting transfers between devices: 49.8 us -> 8.65 us
  between operations: 0.83 us -> 14.9 us
    all_to_all x5 -> x2, waiting for transfers between devices: 518 us -> 1.47 us  [the longest x1 1.47 us: per_device(): lax.all_to_all(back_in.reshape(owners, capacity, width), 'ctx', split_axi...]
    all_gather x0 -> x1, waiting for transfers between devices: none -> 108 us  [per_device(): got = lax.all_gather(plane, 'tp', axis=0, tiled=True)]
    all_to_all x5 -> x2, starting transfers between devices: 49.8 us -> 8.57 us  [the longest x1 4.29 us: per_device(): lax.all_to_all(back_in.reshape(owners, capacity, width), 'ctx', split_axi...]
    reshape x3 -> x4, local copies, waits for them, and re-layouts: 44.2 us -> 3.8 us  [the longest x1 2.05 us: per_device(): back_in.reshape(owners, capacity, width)]
    unnamed x0 -> x1, blocking collectives: none -> 38.9 us
    all_to_all x0 -> x1, blocking collectives: none -> 23.5 us  [per_device(): lax.all_to_all(send.reshape(owners, capacity, -1), 'ctx', split_axis=0, c...]
    reduce_scatter x0 -> x1, waiting for transfers between devices: none -> 19.8 us  [per_device(): lax.psum_scatter(input_part.astype(jnp.bfloat16), 'tp', scatter_dimension...]
    broadcast_in_dim x7 -> x0, local copies, waits for them, and re-layouts: 11.2 us -> none  [the longest x2 5.46 us: per_device(): jnp.broadcast_to(send_in[:, None], (owners, groups, capacity, width))]
  transfers between devices with their start and end apart: 5 -> 4, of which waited for: 4 -> 3; matrix products, arithmetic and copies ran while one was open for 13% -> 11% of each run, Pallas kernels for 0% -> 0%
where the time goes in v1:
time: 297 us; the launch traced here: 296 us
  waiting for transfers between devices  129 us (43%)
  matrix products  71.7 us (24%)
  blocking collectives  62.4 us (21%)
  between operations  14.9 us (5%)
  starting transfers between devices  8.65 us (3%)
  local copies, waits for them, and re-layouts  5.35 us (2%)
  other arithmetic  4.06 us (1%)
    all_gather x1, waiting for transfers between devices, per_device(): got = lax.all_gather(plane, 'tp', axis=0, tiled=True)  108 us
    unnamed x1, blocking collectives  38.9 us
    all_to_all x1, blocking collectives, per_device(): lax.all_to_all(send.reshape(owners, capacity, -1), 'ctx', split_axis=0, c...  23.5 us
    reduce_scatter x1, waiting for transfers between devices, per_device(): lax.psum_scatter(input_part.astype(jnp.bfloat16), 'tp', scatter_dimension...  19.8 us
    dot_general x1, matrix products, expert_grads(): lax.dot_general(rows_in, dg, (((0,), (0,)), ((), ())), preferred_element_...  10 us
    dot_general x1, matrix products, expert_grads(): lax.dot_general(du, wu, (((1,), (1,)), ((), ())), preferred_element_type=...  9.8 us
    dot_general x1, matrix products, expert_grads(): lax.dot_general(rows_in, du, (((0,), (0,)), ((), ())), preferred_element_...  9.52 us
    dot_general x1, matrix products, expert_grads(): lax.dot_general(weighted, rows_grad, (((0,), (0,)), ((), ())), preferred_...  8.14 us
  transfers between devices with their start and end apart: 4, of which 3 were waited for; matrix products, arithmetic and copies ran while one was open for 11% of the time, Pallas kernels for 0%

profile of v1, /device:TPU:0, one launch (start us, length us, event | category | flops | bytes accessed | tf_op | source)
XLA Modules:
  0.0 295.9 jit_solution(15907383244591006829)
XLA Ops:
  7.2 0.8 fusion.24
  8.0 0.8 select_reduce_fusion
  8.9 0.7 multiply_add_fusion
  9.5 0.8 convolution_convert_fusion.6
  10.4 0.3 convolution_convert_fusion.3
  10.7 1.2 convolution_convert_fusion.4
  12.0 0.4 reshape.42
  12.4 23.5 %all_to_all.19 = bf16[8,6,10368]{2,1,0:T(8,128)(2,1)S(1)} all-to-all(bf16[8,6,10368]{2,1,0:T(8,128)(2,1)S(1)} %reshape.42), channel_id=1, replica_groups=mesh['ctx'=8,'tp'=16] {'ctx'}, dimensions={0} | all-to-all | bytes 1990656 | tf_op jit(solution)/shard_map/all_to_all | solution.py:65
  35.9 1.2 reshape.43
  37.1 107.6 %all-gather.2.cloned.1.call-done = bf16[768,10368]{1,0:T(8,128)(2,1)} async-done(((bf16[48,10368]{1,0:T(8,128)(2,1)}), bf16[768,10368]{1,0:T(8,128)(2,1)}) %all-gather.2.cloned.1.call-update) | async-done | bytes 15925264 | tf_op jit(solution)/shard_map/all_gather | solution.py:68
  144.7 1.1 convert_reduce_fusion
  145.8 7.8 %fusion.10 = f32[768,384]{0,1:T(8,128)S(1)} fusion(bf16[768,10368]{1,0:T(8,128)(2,1)} %all-gather.2.cloned.1.call-done, bf16[1,5120,384]{2,1,0:T(8,128)(2,1)} %param.11), kind=kOutput, calls=%fused_computation.15 | convolution fusion | flops 3019898880 | bytes 12976128 | tf_op jit(solution)/shard_map/dot_general | solution.py:17
  153.6 7.1 %fusion.12 = f32[768,384]{0,1:T(8,128)S(1)} fusion(bf16[768,10368]{1,0:T(8,128)(2,1)} %all-gather.2.cloned.1.call-done, bf16[1,5120,384]{2,1,0:T(8,128)(2,1)S(1)} %copy-done.3), kind=kOutput, calls=%fused_computation.17 | convolution fusion | flops 3019898880 | bytes 12976128 | tf_op jit(solution)/shard_map/dot_general | solution.py:18
  160.7 7.4 %multiply_reduce_fusion = (f32[768]{0:T(1024)S(1)}, bf16[768,384]{0,1:T(8,128)(2,1)S(1)}, bf16[768,384]{0,1:T(8,128)(2,1)S(1)}) fusion(f32[768,384]{0,1:T(8,128)S(1)} %fusion.12, f32[768,384]{0,1:T(8,128)S(1)} %fusion.10, f32[768]{0:T(1024)S(1)} %convert_reduce_fusion, bf16[1,384,5120]{2,1,0:T(8,128)(2,1)S(1)} %copy-done.6, ...), kind=kOutput, calls=%fused_computation.26 | convolution fusion | flops 3024911616 | bytes 15341568 | tf_op jit(solution)/shard_map/dot_general | solution.py:24
  168.2 7.9 %fusion.14 = f32[768,5120]{1,0:T(8,128)} fusion(bf16[768,384]{0,1:T(8,128)(2,1)S(1)} %get-tuple-element.6, bf16[1,5120,384]{2,1,0:T(8,128)(2,1)S(1)} %copy-done.2), kind=kOutput, calls=%fused_computation.19 | convolution fusion | flops 3019898880 | bytes 20250624 | tf_op jit(solution)/shard_map/dot_general | solution.py:40
  176.1 9.8 %add_convert_fusion = bf16[768,5120]{1,0:T(8,128)(2,1)} fusion(f32[768,5120]{1,0:T(8,128)} %fusion.14, bf16[768,384]{0,1:T(8,128)(2,1)S(1)} %get-tuple-element.7, bf16[1,5120,384]{2,1,0:T(8,128)(2,1)S(1)} %copy-done.3), kind=kOutput, calls=%fused_computation | convolution fusion | flops 3027763200 | bytes 28114944 | tf_op jit(solution)/shard_map/dot_general | solution.py:43
  186.0 0.6 copy-done.7
  186.6 0.6 dynamic-slice
  187.8 38.9 %all-reduce = f32[768]{0:T(1024)S(1)} all-reduce(f32[768]{0:T(1024)S(1)} %get-tuple-element.5), channel_id=3, replica_groups=mesh['ctx'=8,'tp'=16] {'tp'}, use_global_device_ids=true, to_apply=%region_4.5.clone | all-reduce | flops 768 | bytes 6144
  226.9 0.6 convert.1
  227.5 4.3 %all-to-all-start.2 = ((bf16[8,1,6]{2,1,0:T(2,128)(2,1)}), bf16[8,1,6]{2,1,0:T(2,128)(2,1)S(1)}, u32[]{:S(2)}, u32[]{:S(2)}) async-start(bf16[8,1,6]{2,1,0:T(2,128)(2,1)} %convert.1), calls=%async_computation.3 | async-start | bytes 8192 | tf_op jit(solution)/shard_map/all_to_all | solution.py:84
  231.8 10.0 %fusion.3 = bf16[1,5120,384]{2,1,0:T(8,128)(2,1)} fusion(bf16[768,384]{0,1:T(8,128)(2,1)S(1)} %copy-done.5, bf16[768,10368]{1,0:T(8,128)(2,1)} %all-gather.2.cloned.1.call-done), kind=kOutput, calls=%fused_computation.7 | convolution fusion | flops 3021864960 | bytes 12386304 | tf_op jit(solution)/shard_map/dot_general | solution.py:34
  241.8 8.1 %fusion.5 = bf16[1,384,5120]{2,1,0:T(8,128)(2,1)} fusion(bf16[768,10368]{1,0:T(8,128)(2,1)} %all-gather.2.cloned.1.call-done, f32[768]{0:T(1024)S(1)} %convert_reduce_fusion, f32[768,384]{0,1:T(8,128)S(1)} %copy-done.11, f32[768,384]{0,1:T(8,128)S(1)} %copy-done.9), kind=kOutput, calls=%fused_computation.9 | convolution fusion | flops 3023929344 | bytes 14158848 | tf_op jit(solution)/shard_map/dot_general | solution.py:31
  250.0 19.8 %reduce-scatter.2.cloned.1.call-done = bf16[48,5120]{1,0:T(8,128)(2,1)} async-done(((bf16[768,5120]{1,0:T(8,128)(2,1)}), bf16[48,5120]{1,0:T(8,128)(2,1)}) %reduce-scatter.2.cloned.1.call-update) | async-done | bytes 491536 | tf_op jit(solution)/shard_map/reduce_scatter | solution.py:77
  269.8 2.0 reshape.44
  271.9 4.3 %all-to-all-start.1 = ((bf16[8,6,5120]{2,1,0:T(8,128)(2,1)}), bf16[8,6,5120]{2,1,0:T(8,128)(2,1)S(1)}, u32[]{:S(2)}, u32[]{:S(2)}) async-start(bf16[8,6,5120]{2,1,0:T(8,128)(2,1)} %reshape.44), calls=%async_computation.2 | async-start | bytes 1310720 | tf_op jit(solution)/shard_map/all_to_all | solution.py:81
  276.2 9.5 %fusion.4 = bf16[1,5120,384]{2,1,0:T(8,128)(2,1)} fusion(bf16[768,384]{0,1:T(8,128)(2,1)S(1)} %get-tuple-element.7, bf16[768,10368]{1,0:T(8,128)(2,1)} %all-gather.2.cloned.1.call-done), kind=kOutput, calls=%fused_computation.8 | convolution fusion | flops 3021864960 | bytes 12386304 | tf_op jit(solution)/shard_map/dot_general | solution.py:37
  285.7 0.1 reshape.47
  285.8 0.6 fusion.21
  286.4 1.5 all-to-all-done.1
  287.9 0.2 reshape.45
  288.1 1.0 convolution_convert_fusion.5
  (33 shorter events, 0.5 us)
Async XLA Ops:
  7.2 3.2 %copy-start = (bf16[32,5120]{1,0:T(8,128)(2,1)S(1)}, bf16[32,5120]{1,0:T(8,128)(2,1)}, u32[]{:S(2)}) copy-start(bf16[32,5120]{1,0:T(8,128)(2,1)} %param.8) | copy-start | bytes 983044
  7.2 137.5 %all-gather.2.cloned.1.call-start = ((), (), s32[]{:S(2)}) async-start(), calls=%async_computation.4 | async-start | bytes 16920576 | tf_op jit(solution)/shard_map/all_gather | solution.py:68
  37.1 232.7 %reduce-scatter.2.cloned.1.call-start = ((), (), s32[]{:S(2)}) async-start(), calls=%async_computation.5 | async-start | bytes 8355840 | tf_op jit(solution)/shard_map/reduce_scatter | solution.py:77
  145.8 7.8 %copy-start.3 = (bf16[1,5120,384]{2,1,0:T(8,128)(2,1)S(1)}, bf16[1,5120,384]{2,1,0:T(8,128)(2,1)}, u32[]{:S(2)}) copy-start(bf16[1,5120,384]{2,1,0:T(8,128)(2,1)} %param.12) | copy-start | bytes 11796484
  153.6 7.1 %copy-start.8 = (f32[768,384]{0,1:T(8,128)}, f32[768,384]{0,1:T(8,128)S(1)}, u32[]{:S(2)}) copy-start(f32[768,384]{0,1:T(8,128)S(1)} %fusion.10) | copy-start | bytes 3538948
  153.6 7.1 %copy-start.6 = (bf16[1,384,5120]{2,1,0:T(8,128)(2,1)S(1)}, bf16[1,384,5120]{2,1,0:T(8,128)(2,1)}, u32[]{:S(2)}) copy-start(bf16[1,384,5120]{2,1,0:T(8,128)(2,1)} %param.13) | copy-start | bytes 11796484
  160.7 7.5 %copy-start.10 = (f32[768,384]{0,1:T(8,128)}, f32[768,384]{0,1:T(8,128)S(1)}, u32[]{:S(2)}) copy-start(f32[768,384]{0,1:T(8,128)S(1)} %fusion.12) | copy-start | bytes 3538948
  160.7 7.5 %copy-start.2 = (bf16[1,5120,384]{2,1,0:T(8,128)(2,1)S(1)}, bf16[1,5120,384]{2,1,0:T(8,128)(2,1)}, u32[]{:S(2)}) copy-start(bf16[1,5120,384]{2,1,0:T(8,128)(2,1)} %param.11) | copy-start | bytes 11796484
  168.2 7.9 %copy-start.4 = (bf16[768,384]{0,1:T(8,128)(2,1)}, bf16[768,384]{0,1:T(8,128)(2,1)S(1)}, u32[]{:S(2)}) copy-start(bf16[768,384]{0,1:T(8,128)(2,1)S(1)} %get-tuple-element.6) | copy-start | bytes 1769476
  185.9 0.7 copy-start.7
  185.9 45.8 %copy-start.5 = (bf16[768,384]{0,1:T(8,128)(2,1)S(1)}, bf16[768,384]{0,1:T(8,128)(2,1)}, u32[]{:S(2)}) copy-start(bf16[768,384]{0,1:T(8,128)(2,1)} %copy-done.4) | copy-start | bytes 1769476
  227.5 44.4 %all-to-all-start.2 = ((bf16[8,1,6]{2,1,0:T(2,128)(2,1)}), bf16[8,1,6]{2,1,0:T(2,128)(2,1)S(1)}, u32[]{:S(2)}, u32[]{:S(2)}) async-start(bf16[8,1,6]{2,1,0:T(2,128)(2,1)} %convert.1), calls=%async_computation.3 | async-start | bytes 8192 | tf_op jit(solution)/shard_map/all_to_all | solution.py:84
  231.8 10.0 %copy-start.9 = (f32[768,384]{0,1:T(8,128)S(1)}, f32[768,384]{0,1:T(8,128)}, u32[]{:S(2)}) copy-start(f32[768,384]{0,1:T(8,128)} %copy-done.8) | copy-start | bytes 3538948
  231.8 10.0 %copy-start.11 = (f32[768,384]{0,1:T(8,128)S(1)}, f32[768,384]{0,1:T(8,128)}, u32[]{:S(2)}) copy-start(f32[768,384]{0,1:T(8,128)} %copy-done.10) | copy-start | bytes 3538948
  271.9 16.0 %all-to-all-start.1 = ((bf16[8,6,5120]{2,1,0:T(8,128)(2,1)}), bf16[8,6,5120]{2,1,0:T(8,128)(2,1)S(1)}, u32[]{:S(2)}, u32[]{:S(2)}) async-start(bf16[8,6,5120]{2,1,0:T(8,128)(2,1)} %reshape.44), calls=%async_computation.2 | async-start | bytes 1310720 | tf_op jit(solution)/shard_map/all_to_all | solution.py:81
  276.1 13.0 %copy-start.1 = (bf16[32,5120]{1,0:T(8,128)(2,1)S(1)}, bf16[32,5120]{1,0:T(8,128)(2,1)}, u32[]{:S(2)}) copy-start(bf16[32,5120]{1,0:T(8,128)(2,1)} %param.8) | copy-start | bytes 983044
Sparse Core Ops, SparseCore 0:
  37.2 107.4 all-gather.1
  186.1 83.6 reduce-scatter.1

commit v2 on v1

v2 whole, which is shorter than its diff:
```python
import jax
import jax.numpy as jnp
from jax import lax
from jax.experimental import pallas as pl
from jax.experimental.pallas import tpu as pltpu
from jax.sharding import PartitionSpec as P

F32 = jnp.float32
BF16 = jnp.bfloat16
SIDE = 4
OWNERS = 8
PAIR = 2
CHUNKS = 3
CAPACITY = PAIR * CHUNKS
BLOCK = OWNERS * PAIR
ROWS = SIDE * SIDE * BLOCK
LANES = 128


def dot(a, b):
    return jnp.dot(a, b, preferred_element_type=F32)


def dot_nt(a, b):
    return lax.dot_general(a, b, (((1,), (1,)), ((), ())), preferred_element_type=F32)


def dot_tn(a, b):
    return lax.dot_general(a, b, (((0,), (0,)), ((), ())), preferred_element_type=F32)


def iota(shape, dim):
    return lax.broadcasted_iota(jnp.int32, shape, dim)


def select(mask):
    return jnp.where(mask, 1.0, 0.0).astype(BF16)


def kernel(
    tokens, grads, prob, ids, wg_in, wu_in, wd_in,
    out_tokens, out_prob, out_wg, out_wu, out_wd,
    wg, wu, wd, snd, rcv, ga, gb, part, s1, s2, t1, t2, fin, rsnd, rrcv,
    acc, dd, wei, pps, ppr,
    w_sem, o_sem, p1_send, p1_recv, ag_send, ag_recv, rs_send, rs_recv,
    pp_send, pp_recv, rt_send, rt_recv,
):
    count, width = tokens.shape
    units = wg.shape[1]
    quarter, eighth, half = width // 4, width // 8, width // 2
    c = lax.axis_index("ctx")
    t = lax.axis_index("tp")
    x, z = t // SIDE, t % SIDE

    def at_xz(xd, zd):
        return {"ctx": c, "tp": xd * SIDE + zd}

    def step(p, by):
        return (p + by + SIDE) % SIDE

    barrier = pltpu.get_barrier_semaphore()
    for dc in range(1, OWNERS):
        pl.semaphore_signal(
            barrier, inc=1, device_id={"ctx": (c + dc) % OWNERS, "tp": t},
            device_id_type=pl.DeviceIdType.MESH,
        )
    for d in range(1, SIDE * SIDE):
        pl.semaphore_signal(
            barrier, inc=1, device_id=at_xz(step(x, d // SIDE), step(z, d % SIDE)),
            device_id_type=pl.DeviceIdType.MESH,
        )

    loads = [
        pltpu.make_async_copy(src, dst, w_sem.at[i])
        for i, (src, dst) in enumerate(((wg_in.at[0], wg), (wu_in.at[0], wu), (wd_in.at[0], wd)))
    ]
    for copy in loads:
        copy.start()

    sent = []

    def send(src, dst, send_sem, recv_sem, device):
        copy = pltpu.make_async_remote_copy(
            src_ref=src, dst_ref=dst, send_sem=send_sem, recv_sem=recv_sem,
            device_id=device, device_id_type=pl.DeviceIdType.MESH,
        )
        copy.start()
        sent.append(copy)
        return copy

    onehot = jnp.where(ids[...] == iota((count, LANES), 1), 1.0, 0.0)
    lower = select(iota((count, count), 0) >= iota((count, count), 1))
    ranks = dot(lower, onehot.astype(BF16))
    slot = jnp.sum(ranks * onehot, axis=1, keepdims=True) - 1.0
    target = ids[...].astype(F32) * CAPACITY + slot
    eye = iota((count, count), 0) == iota((count, count), 1)
    target_row = jnp.sum(
        jnp.where(eye, jnp.broadcast_to(target, (count, count)), 0.0), axis=0, keepdims=True
    )
    prob_col = jnp.sum(
        jnp.where(eye, jnp.broadcast_to(prob[...].astype(F32), (count, count)), 0.0),
        axis=1, keepdims=True,
    )
    prob_wide = jnp.broadcast_to(prob_col, (count, LANES)).astype(BF16)
    slots = OWNERS * BLOCK

    def build(k):
        row = iota((slots, count), 0)
        inner = row % BLOCK
        want = (row // BLOCK) * CAPACITY + PAIR * k + inner % PAIR
        hit = jnp.broadcast_to(target_row, (slots, count)) == want.astype(F32)
        of_x = (inner // PAIR) % 2 == 0
        total = jnp.zeros((slots, quarter), F32)
        for q in range(4):
            mine = hit & (inner // 4 == q)
            cols = slice(q * quarter, (q + 1) * quarter)
            total += dot(select(mine & of_x), tokens[:, cols])
            total += dot(select(mine & ~of_x), grads[:, cols])
        snd[k, :, :, :quarter] = total.astype(BF16).reshape(OWNERS, BLOCK, quarter)
        probs = dot(select(hit & of_x & (inner // 4 == 0)), prob_wide)
        snd[k, :, :, quarter:] = probs.astype(BF16).reshape(OWNERS, BLOCK, LANES)

    p1 = {}

    def disperse(k):
        for dc in range(1, OWNERS):
            to = (c + dc) % OWNERS
            p1[k, dc] = send(
                snd.at[k, to], rcv.at[k, c], p1_send.at[k, dc], p1_recv.at[k, dc],
                {"ctx": to, "tp": t},
            )
        rcv[k, c] = snd[k, c]

    def assemble(k):
        for dc in range(1, OWNERS):
            p1[k, dc].wait_recv()
        row = iota((2 * BLOCK, slots), 0)
        col = iota((2 * BLOCK, slots), 1)
        one = row % BLOCK
        for q in range(4):
            where = (one // PAIR) * BLOCK + q * 4 + (row // BLOCK) * PAIR + one % PAIR
            pick = select(col == where)
            got = dot(pick, rcv[k, :, :, :quarter].reshape(slots, quarter)).astype(BF16)
            cols = slice(q * quarter, (q + 1) * quarter)
            ga[k, z, x, :, cols] = got[:BLOCK]
            gb[k, z, x, :, cols] = got[BLOCK:]
            if q == 0:
                probs = dot(pick, rcv[k, :, :, quarter:].reshape(slots, LANES)).astype(BF16)
                ga[k, z, x, :, width:] = probs[:BLOCK]

    ag = {}
    halves = (
        (pl.ds(0, half), pl.ds(half, half + LANES)),
        (pl.ds(0, half), pl.ds(half, half)),
    )

    def ag_send_one(k, arr, n, ref, device):
        ag[k, arr, n] = send(ref, ref, ag_send.at[k, arr, n], ag_recv.at[k, arr, n], device)

    def near(arr, stage, by):
        along_x = (arr == 0) == (stage == 1)
        return at_xz(step(x, by), z) if along_x else at_xz(x, step(z, by))

    def single(k, arr, by, cols=None):
        buf = (ga, gb)[arr]
        xd, zd = (step(x, by), z) if arr == 0 else (x, step(z, by))
        return buf.at[k, zd, xd] if cols is None else buf.at[k, zd, xd, :, cols]

    def slab(k, arr, by, cols=None):
        if arr == 0:
            zd = step(z, by)
            return ga.at[k, zd] if cols is None else ga.at[k, zd, :, :, cols]
        xd = step(x, by)
        return gb.at[k, :, xd] if cols is None else gb.at[k, :, xd, :, cols]

    def g1(k):
        for arr in range(2):
            ag_send_one(k, arr, 0, single(k, arr, 0), near(arr, 1, 1))
            ag_send_one(k, arr, 1, single(k, arr, 0), near(arr, 1, -1))

    def g2(k):
        for arr in range(2):
            ag[k, arr, 0].wait_recv()
            ag_send_one(k, arr, 2, single(k, arr, -1, halves[arr][0]), near(arr, 1, 1))
            ag[k, arr, 1].wait_recv()
            ag_send_one(k, arr, 3, single(k, arr, 1, halves[arr][1]), near(arr, 1, -1))

    def g3(k):
        for arr in range(2):
            ag[k, arr, 2].wait_recv()
            ag[k, arr, 3].wait_recv()
            ag_send_one(k, arr, 4, slab(k, arr, 0), near(arr, 2, 1))
            ag_send_one(k, arr, 5, slab(k, arr, 0), near(arr, 2, -1))

    def g4(k):
        for arr in range(2):
            ag[k, arr, 4].wait_recv()
            ag_send_one(k, arr, 6, slab(k, arr, -1, halves[arr][0]), near(arr, 2, 1))
        for arr in range(2):
            ag[k, arr, 5].wait_recv()
            ag_send_one(k, arr, 7, slab(k, arr, 1, halves[arr][1]), near(arr, 2, -1))

    def g5(k):
        for arr in range(2):
            ag[k, arr, 6].wait_recv()
            ag[k, arr, 7].wait_recv()

    deep = quarter
    wide = width // 10

    def forward(k):
        def products(i, first):
            at = pl.ds(pl.multiple_of(i * deep, deep), deep)
            rows_in = ga[k, :, :, :, at].reshape(ROWS, deep)
            rows_grad = gb[k, :, :, :, at].reshape(ROWS, deep)
            for n, value in enumerate((
                lambda: dot(rows_in, wg[at, :]),
                lambda: dot(rows_in, wu[at, :]),
                lambda: dot_nt(rows_grad, wd[:, at]),
            )):
                acc[n] = value() if first else acc[n] + value()

        products(0, True)

        @pl.loop(1, width // deep)
        def _(i):
            products(i, False)

        part_rows = 2 * LANES // 4

        @pl.loop(0, ROWS // part_rows)
        def _(i):
            at = pl.ds(pl.multiple_of(i * part_rows, part_rows), part_rows)
            keep = pl.ds(pl.multiple_of(k * ROWS + i * part_rows, part_rows), part_rows)
            g, u, raw = acc[0, at, :], acc[1, at, :], acc[2, at, :]
            sig = jax.nn.sigmoid(g)
            act = g * sig
            hidden = act * u
            probs = ga[k, i, :, :, width:].reshape(part_rows, LANES).astype(F32)[:, :1]
            wei[keep, :] = (probs * hidden).astype(BF16)
            dh = probs * raw
            dd[keep, :units] = (dh * u * sig * (1.0 + g * (1.0 - sig))).astype(BF16)
            dd[keep, units:] = (dh * act).astype(BF16)
            sums = jnp.broadcast_to(
                jnp.sum(hidden * raw, axis=1, keepdims=True), (part_rows, LANES)
            )
            spot = iota((part_rows, LANES), 1) == k * BLOCK + iota((part_rows, LANES), 0) % BLOCK
            lanes = jnp.sum(
                jnp.where(spot, sums, 0.0).reshape(SIDE, BLOCK, LANES), axis=1, keepdims=True
            )
            lanes = jnp.broadcast_to(lanes, (SIDE, 8, LANES))
            pps[i] = lanes if k == 0 else pps[i] + lanes

    def backward(k):
        dg = dd[k * ROWS:(k + 1) * ROWS, :units]
        du = dd[k * ROWS:(k + 1) * ROWS, units:]

        @pl.loop(0, width // wide)
        def _(i):
            at = pl.ds(pl.multiple_of(i * wide, wide), wide)
            value = dot_nt(dg, wg[at, :]) + dot_nt(du, wu[at, :])
            part[k, :, :, :, at] = value.astype(BF16).reshape(SIDE, SIDE, BLOCK, wide)

    rs = {}

    def rs_send_one(k, h, n, src, dst, device):
        rs[k, h, n] = send(src, dst, rs_send.at[k, h, n], rs_recv.at[k, h, n], device)

    def cols_of(h, piece):
        if piece is None:
            return slice(h * half, (h + 1) * half)
        return slice(h * half + piece * quarter, h * half + (piece + 1) * quarter)

    def group(h, by):
        return (step(z, by), slice(None)) if h == 0 else (slice(None), step(x, by))

    def own(h, by):
        return (z, step(x, by)) if h == 0 else (step(z, by), x)

    def add_into(where, others):
        value = part[where].astype(F32)
        for other in others:
            value += other[...].astype(F32)
        part[where] = value.astype(BF16)

    def r1(k):
        for h in range(2):
            far = group(h, 2)
            rs_send_one(k, h, 0, part.at[(k,) + far + (slice(None), cols_of(h, 0))],
                        s1.at[k, h, 0], near(h, 2, 1))
            rs_send_one(k, h, 1, part.at[(k,) + far + (slice(None), cols_of(h, 1))],
                        s1.at[k, h, 1], near(h, 2, -1))

    def r2(k):
        for h in range(2):
            for side, by in ((0, 1), (1, -1)):
                rs[k, h, side].wait_recv()
                to = (k,) + group(h, by) + (slice(None),)
                add_into(to + (cols_of(h, side),), (s1.at[k, h, side],))
                rs_send_one(k, h, 2 + side, part.at[to + (cols_of(h, None),)],
                            s2.at[k, h, side], near(h, 2, by))

    def r3(k):
        for h in range(2):
            rs[k, h, 2].wait_recv()
            rs[k, h, 3].wait_recv()
            far = (k,) + own(h, 2) + (slice(None),)
            mine = (k,) + group(h, 0) + (slice(None), cols_of(h, None))
            add_into(mine, (s2.at[k, h, 0], s2.at[k, h, 1]))
            rs_send_one(k, h, 4, part.at[far + (cols_of(h, 0),)], t1.at[k, h, 0], near(h, 1, 1))
            rs_send_one(k, h, 5, part.at[far + (cols_of(h, 1),)], t1.at[k, h, 1], near(h, 1, -1))

    def r4(k):
        for h in range(2):
            for side, by in ((0, 1), (1, -1)):
                rs[k, h, 4 + side].wait_recv()
                to = (k,) + own(h, by) + (slice(None),)
                add_into(to + (cols_of(h, side),), (t1.at[k, h, side],))
                rs_send_one(k, h, 6 + side, part.at[to + (cols_of(h, None),)],
                            t2.at[k, h, side], near(h, 1, by))

    rt = {}

    def r5(k):
        for h in range(2):
            rs[k, h, 6].wait_recv()
            rs[k, h, 7].wait_recv()
            value = part[(k, z, x, slice(None), cols_of(h, None))].astype(F32)
            value += t2[k, h, 0].astype(F32) + t2[k, h, 1].astype(F32)
            fin[:, cols_of(h, None)] = value.astype(BF16)
        row = iota((slots, BLOCK), 0)
        inner = row % BLOCK
        home = iota((slots, BLOCK), 1) == (row // BLOCK) * PAIR + inner % PAIR
        total = jnp.zeros((slots, eighth), F32)
        for q in range(8):
            total += dot(select(home & (inner // PAIR == q)), fin[:, q * eighth:(q + 1) * eighth])
        rsnd[k, :, :, :eighth] = total.astype(BF16).reshape(OWNERS, BLOCK, eighth)
        span = pl.ds(0, eighth)
        if k == CHUNKS - 1:
            span = pl.ds(0, eighth + LANES)
            for d in range(1, SIDE * SIDE):
                pp[d].wait_recv()
            ppr[0] = pps[z, x]
            summed = jnp.sum(ppr[...], axis=0)[:1]
            held = CHUNKS * BLOCK
            diagonal = iota((held, LANES), 0) == iota((held, LANES), 1)
            column = jnp.sum(
                jnp.where(diagonal, jnp.broadcast_to(summed, (held, LANES)), 0.0),
                axis=1, keepdims=True,
            )
            column = jnp.broadcast_to(column, (held, LANES)).astype(BF16)
            row = iota((slots, held), 0)
            inner = row % BLOCK
            place = (inner // PAIR) * BLOCK + (row // BLOCK) * PAIR + inner % PAIR
            probs = dot(select(iota((slots, held), 1) == place), column)
            rsnd[k, :, :, eighth:] = probs.astype(BF16).reshape(OWNERS, BLOCK, LANES)
        for dc in range(1, OWNERS):
            to = (c + dc) % OWNERS
            rt[k, dc] = send(
                rsnd.at[k, to, :, span], rrcv.at[k, c, :, span],
                rt_send.at[k, dc], rt_recv.at[k, dc], {"ctx": to, "tp": t},
            )
        rrcv[k, c] = rsnd[k, c]

    pp = {}

    def probs_out():
        for d in range(1, SIDE * SIDE):
            xd, zd = step(x, d // SIDE), step(z, d % SIDE)
            pp[d] = send(pps.at[zd, xd], ppr.at[d], pp_send.at[d], pp_recv.at[d], at_xz(xd, zd))

    def weight_in(first, last):
        @pl.loop(first, last)
        def _(i):
            at = pl.ds(pl.multiple_of(i * wide, wide), wide)
            rows_in = ga[:, :, :, :, at].reshape(CHUNKS * ROWS, wide)
            value = dot_tn(rows_in, dd[...])
            wg[at, :] = value[:, :units].astype(BF16)
            wu[at, :] = value[:, units:].astype(BF16)

    def weight_down():
        @pl.loop(0, width // wide)
        def _(i):
            at = pl.ds(pl.multiple_of(i * wide, wide), wide)
            rows_grad = gb[:, :, :, :, at].reshape(CHUNKS * ROWS, wide)
            wd[:, at] = dot_tn(wei[...], rows_grad).astype(BF16)

    stores = [
        pltpu.make_async_copy(src, dst, o_sem.at[i])
        for i, (src, dst) in enumerate(
            ((wg, out_wg.at[0]), (wu, out_wu.at[0]), (wd, out_wd.at[0]))
        )
    ]

    build(0)
    pl.semaphore_wait(barrier, OWNERS - 1 + SIDE * SIDE - 1)
    disperse(0)
    build(1)
    disperse(1)
    build(2)
    disperse(2)
    assemble(0)
    g1(0)
    assemble(1)
    g1(1)
    g2(0)
    assemble(2)
    g1(2)
    g3(0)
    g2(1)
    g3(1)
    g2(2)
    g4(0)
    g3(2)
    for copy in loads:
        copy.wait()
    g5(0)
    forward(0)
    backward(0)
    r1(0)
    g4(1)
    r2(0)
    g5(1)
    g4(2)
    forward(1)
    backward(1)
    r1(1)
    r3(0)
    r2(1)
    r4(0)
    g5(2)
    forward(2)
    backward(2)
    r1(2)
    probs_out()
    r3(1)
    r5(0)
    weight_in(0, 3)
    r2(2)
    r4(1)
    weight_in(3, 6)
    r3(2)
    r5(1)
    weight_in(6, 8)
    r4(2)
    weight_in(8, 10)
    stores[0].start()
    stores[1].start()
    r5(2)
    weight_down()
    stores[2].start()

    for k in range(CHUNKS):
        for dc in range(1, OWNERS):
            rt[k, dc].wait_recv()
    row = iota((count, slots), 1)
    inner = row % BLOCK
    base = (row // BLOCK) * CAPACITY + inner % PAIR
    hits = [
        jnp.broadcast_to(target, (count, slots)) == (base + PAIR * k).astype(F32)
        for k in range(CHUNKS)
    ]
    for q in range(8):
        total = jnp.zeros((count, eighth), F32)
        for k in range(CHUNKS):
            total += dot(
                select(hits[k] & (inner // PAIR == q)),
                rrcv[k, :, :, :eighth].reshape(slots, eighth),
            )
        out_tokens[:, q * eighth:(q + 1) * eighth] = total.astype(BF16)
    total = jnp.zeros((count, LANES), F32)
    for k in range(CHUNKS):
        total += dot(
            select(hits[k] & (inner // PAIR == k)),
            rrcv[CHUNKS - 1, :, :, eighth:].reshape(slots, LANES),
        )
    out_prob[...] = total.astype(BF16)

    for copy in sent:
        copy.wait_send()
    for copy in stores:
        copy.wait()


def per_device(tokens, grad_out, gate_prob, expert_ids, w_gate, w_up, w_down):
    count, width = tokens.shape
    units = w_gate.shape[2]
    quarter, eighth, half = width // 4, width // 8, width // 2
    vmem = pl.BlockSpec(memory_space=pltpu.VMEM)
    anywhere = pl.BlockSpec(memory_space=pl.ANY)
    rows = CHUNKS * ROWS
    dma = pltpu.SemaphoreType.DMA
    grad_tokens, grad_prob, grad_wg, grad_wu, grad_wd = pl.pallas_call(
        kernel,
        out_shape=(
            jax.ShapeDtypeStruct((count, width), BF16),
            jax.ShapeDtypeStruct((count, LANES), BF16),
            jax.ShapeDtypeStruct(w_gate.shape, BF16),
            jax.ShapeDtypeStruct(w_up.shape, BF16),
            jax.ShapeDtypeStruct(w_down.shape, BF16),
        ),
        in_specs=[vmem] * 4 + [anywhere] * 3,
        out_specs=[vmem] * 2 + [anywhere] * 3,
        scratch_shapes=[
            pltpu.VMEM((width, units), BF16),
            pltpu.VMEM((width, units), BF16),
            pltpu.VMEM((units, width), BF16),
            pltpu.VMEM((CHUNKS, OWNERS, BLOCK, quarter + LANES), BF16),
            pltpu.VMEM((CHUNKS, OWNERS, BLOCK, quarter + LANES), BF16),
            pltpu.VMEM((CHUNKS, SIDE, SIDE, BLOCK, width + LANES), BF16),
            pltpu.VMEM((CHUNKS, SIDE, SIDE, BLOCK, width), BF16),
            pltpu.VMEM((CHUNKS, SIDE, SIDE, BLOCK, width), BF16),
            pltpu.VMEM((CHUNKS, 2, 2, SIDE, BLOCK, quarter), BF16),
            pltpu.VMEM((CHUNKS, 2, 2, SIDE, BLOCK, half), BF16),
            pltpu.VMEM((CHUNKS, 2, 2, BLOCK, quarter), BF16),
            pltpu.VMEM((CHUNKS, 2, 2, BLOCK, half), BF16),
            pltpu.VMEM((BLOCK, width), BF16),
            pltpu.VMEM((CHUNKS, OWNERS, BLOCK, eighth + LANES), BF16),
            pltpu.VMEM((CHUNKS, OWNERS, BLOCK, eighth + LANES), BF16),
            pltpu.VMEM((3, ROWS, units), F32),
            pltpu.VMEM((rows, 2 * units), BF16),
            pltpu.VMEM((rows, units), BF16),
            pltpu.VMEM((SIDE, SIDE, 8, LANES), F32),
            pltpu.VMEM((SIDE * SIDE, 8, LANES), F32),
            dma((3,)),
            dma((3,)),
            dma((CHUNKS, OWNERS)),
            dma((CHUNKS, OWNERS)),
            dma((CHUNKS, 2, 8)),
            dma((CHUNKS, 2, 8)),
            dma((CHUNKS, 2, 8)),
            dma((CHUNKS, 2, 8)),
            dma((SIDE * SIDE,)),
            dma((SIDE * SIDE,)),
            dma((CHUNKS, OWNERS)),
            dma((CHUNKS, OWNERS)),
        ],
        compiler_params=pltpu.CompilerParams(
            collective_id=0, has_side_effects=True, vmem_limit_bytes=60 * 2**20
        ),
    )(tokens, grad_out, gate_prob[None], expert_ids, w_gate, w_up, w_down)
    return grad_tokens, grad_prob[:, 0], grad_wg, grad_wu, grad_wd


def solution(mesh):
    in_specs = (
        P(("ctx", "tp"), None),
        P(("ctx", "tp"), None),
        P(("ctx", "tp")),
        P(("ctx", "tp"), None),
        P("ctx", None, "tp"),
        P("ctx", None, "tp"),
        P("ctx", "tp", None),
    )
    out_specs = (
        P(("ctx", "tp"), None),
        P(("ctx", "tp")),
        P("ctx", None, "tp"),
        P("ctx", None, "tp"),
        P("ctx", "tp", None),
    )
    return jax.shard_map(
        per_device, mesh=mesh, in_specs=in_specs, out_specs=out_specs, check_vma=False
    )
```

time: 297 us -> 178 us (0.60)
  Pallas kernels: 0 us -> 162 us
  waiting for transfers between devices: 129 us -> 0 us
  matrix products: 71.7 us -> 0 us
  blocking collectives: 62.4 us -> 0 us
  between operations: 14.9 us -> 0.64 us
  local copies, waits for them, and re-layouts: 5.35 us -> 14.4 us
  starting transfers between devices: 8.65 us -> 0 us
  other arithmetic: 4.06 us -> 0 us
    pallas_call x0 -> x1, Pallas kernels: none -> 162 us  [per_device(): pl.pallas_call(kernel, out_shape=(jax.ShapeDtypeStruct((count, width), BF...]
    all_gather x1 -> x0, waiting for transfers between devices: 108 us -> none  [per_device(): got = lax.all_gather(plane, 'tp', axis=0, tiled=True)]
    dot_general x13 -> x0, matrix products: 71.7 us -> none  [the longest x1 10 us: expert_grads(): lax.dot_general(rows_in, dg, (((0,), (0,)), ((), ())), preferred_element_...]
    unnamed x1 -> x0, blocking collectives: 38.9 us -> none
    all_to_all x1 -> x0, blocking collectives: 23.5 us -> none  [per_device(): lax.all_to_all(send.reshape(owners, capacity, -1), 'ctx', split_axis=0, c...]
    reduce_scatter x1 -> x0, waiting for transfers between devices: 19.8 us -> none  [per_device(): lax.psum_scatter(input_part.astype(jnp.bfloat16), 'tp', scatter_dimension...]
    unnamed x26 -> x9, local copies, waits for them, and re-layouts: 1.35 us -> 13.1 us
    all_to_all x2 -> x0, starting transfers between devices: 8.57 us -> none  [the longest x1 4.29 us: per_device(): lax.all_to_all(back_in.reshape(owners, capacity, width), 'ctx', split_axi...]
  transfers between devices with their start and end apart: 4 -> 0, of which waited for: 3 -> 0; matrix products, arithmetic and copies ran while one was open for 11% -> 0% of each run, Pallas kernels for 0% -> 0%
where the time goes in v2:
time: 178 us
  Pallas kernels  162 us (91%)
  local copies, waits for them, and re-layouts  14.4 us (8%)
    pallas_call x1, Pallas kernels, per_device(): pl.pallas_call(kernel, out_shape=(jax.ShapeDtypeStruct((count, width), BF...  162 us
    unnamed x9, local copies, waits for them, and re-layouts  13.1 us

profile of v2, /device:TPU:0, one launch (start us, length us, event | category | flops | bytes accessed | tf_op | source)
XLA Modules:
  0.0 177.6 jit_solution(7118774075997628843)
XLA Ops:
  0.6 1.3 copy.13.ids
  2.0 162.5 %shard_map.110 = (bf16[32,5120]{1,0:T(8,128)(2,1)}, bf16[32,128]{1,0:T(8,128)(2,1)}, bf16[1,5120,384]{2,1,0:T(8,128)(2,1)}, bf16[1,5120,384]{2,1,0:T(8,128)(2,1)}, bf16[1,384,5120]{2,1,0:T(8,128)(2,1)}) custom-call(bf16[32,5120]{1,0:T(8,128)(2,1)} %tokens.1, bf16[32,5120]{1,0:T(8,128)(2,1)} %grads.1, bf16[1,32]{1,0:T(2,128)(2,1)} %bitcast.1, ...), custom_call_target="tpu_custom_call" | custom-call | tf_op jit(solution)/shard_map/pallas_call | solution.py:493
  164.5 1.3 slice_reduce_fusion
  165.8 1.7 copy.18
  167.5 0.0 copy-start.1
  167.5 4.6 %copy.19 = bf16[1,5120,384]{2,1,0:T(8,128)(2,1)} copy(bf16[1,5120,384]{2,1,0:T(8,128)(2,1)} %get-tuple-element.22) | data formatting | bytes 7864320
  172.1 0.0 copy-done.1
  172.1 0.0 copy-start
  172.1 2.0 %copy.20 = bf16[1,5120,384]{2,1,0:T(8,128)(2,1)} copy(bf16[1,5120,384]{2,1,0:T(8,128)(2,1)S(1)} %copy-done.1) | data formatting | bytes 7864320
  174.1 1.5 copy-done
  175.6 1.9 %copy.21 = bf16[1,384,5120]{2,1,0:T(8,128)(2,1)} copy(bf16[1,384,5120]{2,1,0:T(8,128)(2,1)S(1)} %copy-done) | data formatting | bytes 7864320
Async XLA Ops:
  167.5 4.6 %copy-start.1 = (bf16[1,5120,384]{2,1,0:T(8,128)(2,1)S(1)}, bf16[1,5120,384]{2,1,0:T(8,128)(2,1)}, u32[]{:S(2)}) copy-start(bf16[1,5120,384]{2,1,0:T(8,128)(2,1)} %get-tuple-element.23) | copy-start | bytes 11796484
  172.1 3.5 %copy-start = (bf16[1,384,5120]{2,1,0:T(8,128)(2,1)S(1)}, bf16[1,384,5120]{2,1,0:T(8,128)(2,1)}, u32[]{:S(2)}) copy-start(bf16[1,384,5120]{2,1,0:T(8,128)(2,1)} %get-tuple-element.24) | copy-start | bytes 11796484

commit v3 on v2

--- a/solution.py
+++ b/solution.py
@@ -40,12 +40,13 @@
 def kernel(
     tokens, grads, prob, ids, wg_in, wu_in, wd_in,
     out_tokens, out_prob, out_wg, out_wu, out_wd,
-    wg, wu, wd, snd, rcv, ga, gb, part, s1, s2, t1, t2, fin, rsnd, rrcv,
+    stk, snd, rcv, ga, gb, part, s1, s2, t1, t2, fin, rsnd, rrcv,
     acc, dd, wei, pps, ppr,
-    w_sem, o_sem, p1_send, p1_recv, ag_send, ag_recv, rs_send, rs_recv,
+    i_sem, w_sem, p1_send, p1_recv, ag_send, ag_recv, rs_send, rs_recv,
     pp_send, pp_recv, rt_send, rt_recv,
 ):
     count, width = tokens.shape
+    wg, wu, wd = out_wg.at[0], out_wu.at[0], out_wd.at[0]
     units = wg.shape[1]
     quarter, eighth, half = width // 4, width // 8, width // 2
     c = lax.axis_index("ctx")
@@ -70,6 +71,17 @@
             device_id_type=pl.DeviceIdType.MESH,
         )
 
+    stacking = [
+        pltpu.make_async_copy(
+            src.at[:, q * quarter:(q + 1) * quarter],
+            stk.at[pl.ds((2 * q + n) * count, count), pl.ds(0, quarter)],
+            i_sem.at[2 * q + n],
+        )
+        for q in range(4)
+        for n, src in enumerate((tokens, grads))
+    ]
+    for copy in stacking:
+        copy.start()
     loads = [
         pltpu.make_async_copy(src, dst, w_sem.at[i])
         for i, (src, dst) in enumerate(((wg_in.at[0], wg), (wu_in.at[0], wu), (wd_in.at[0], wd)))
@@ -88,37 +100,37 @@
         sent.append(copy)
         return copy
 
-    onehot = jnp.where(ids[...] == iota((count, LANES), 1), 1.0, 0.0)
+    deck = 8 * count
+
+    def column(line):
+        eye = iota((count, count), 0) == iota((count, count), 1)
+        spread = jnp.broadcast_to(line[...].astype(F32), (count, count))
+        return jnp.sum(jnp.where(eye, spread, 0.0), axis=1, keepdims=True)
+
+    chosen = column(ids)
+    onehot = jnp.where(chosen == iota((count, LANES), 1).astype(F32), 1.0, 0.0)
     lower = select(iota((count, count), 0) >= iota((count, count), 1))
     ranks = dot(lower, onehot.astype(BF16))
     slot = jnp.sum(ranks * onehot, axis=1, keepdims=True) - 1.0
-    target = ids[...].astype(F32) * CAPACITY + slot
-    eye = iota((count, count), 0) == iota((count, count), 1)
+    target = chosen * CAPACITY + slot
     target_row = jnp.sum(
-        jnp.where(eye, jnp.broadcast_to(target, (count, count)), 0.0), axis=0, keepdims=True
+        jnp.where(
+            iota((count, deck), 0) == iota((count, deck), 1) % count,
+            jnp.broadcast_to(target, (count, deck)), 0.0,
+        ),
+        axis=0, keepdims=True,
     )
-    prob_col = jnp.sum(
-        jnp.where(eye, jnp.broadcast_to(prob[...].astype(F32), (count, count)), 0.0),
-        axis=1, keepdims=True,
-    )
-    prob_wide = jnp.broadcast_to(prob_col, (count, LANES)).astype(BF16)
+    stk[:, quarter:] = jnp.zeros((deck, LANES), BF16)
+    stk[:count, quarter:] = jnp.broadcast_to(column(prob), (count, LANES)).astype(BF16)
     slots = OWNERS * BLOCK
 
     def build(k):
-        row = iota((slots, count), 0)
+        row, col = iota((slots, deck), 0), iota((slots, deck), 1)
         inner = row % BLOCK
         want = (row // BLOCK) * CAPACITY + PAIR * k + inner % PAIR
-        hit = jnp.broadcast_to(target_row, (slots, count)) == want.astype(F32)
-        of_x = (inner // PAIR) % 2 == 0
-        total = jnp.zeros((slots, quarter), F32)
-        for q in range(4):
-            mine = hit & (inner // 4 == q)
-            cols = slice(q * quarter, (q + 1) * quarter)
-            total += dot(select(mine & of_x), tokens[:, cols])
-            total += dot(select(mine & ~of_x), grads[:, cols])
-        snd[k, :, :, :quarter] = total.astype(BF16).reshape(OWNERS, BLOCK, quarter)
-        probs = dot(select(hit & of_x & (inner // 4 == 0)), prob_wide)
-        snd[k, :, :, quarter:] = probs.astype(BF16).reshape(OWNERS, BLOCK, LANES)
+        hit = jnp.broadcast_to(target_row, (slots, deck)) == want.astype(F32)
+        pick = select(hit & (inner // PAIR == col // count))
+        snd[k] = dot(pick, stk[...]).astype(BF16).reshape(OWNERS, BLOCK, quarter + LANES)
 
     p1 = {}
 
@@ -134,19 +146,15 @@
     def assemble(k):
         for dc in range(1, OWNERS):
             p1[k, dc].wait_recv()
-        row = iota((2 * BLOCK, slots), 0)
-        col = iota((2 * BLOCK, slots), 1)
+        row, col = iota((slots, slots), 0), iota((slots, slots), 1)
         one = row % BLOCK
+        where = (one // PAIR) * BLOCK + (row // BLOCK) * PAIR + one % PAIR
+        got = dot(select(col == where), rcv[k].reshape(slots, quarter + LANES)).astype(BF16)
         for q in range(4):
-            where = (one // PAIR) * BLOCK + q * 4 + (row // BLOCK) * PAIR + one % PAIR
-            pick = select(col == where)
-            got = dot(pick, rcv[k, :, :, :quarter].reshape(slots, quarter)).astype(BF16)
             cols = slice(q * quarter, (q + 1) * quarter)
-            ga[k, z, x, :, cols] = got[:BLOCK]
-            gb[k, z, x, :, cols] = got[BLOCK:]
-            if q == 0:
-                probs = dot(pick, rcv[k, :, :, quarter:].reshape(slots, LANES)).astype(BF16)
-                ga[k, z, x, :, width:] = probs[:BLOCK]
+            ga[k, z, x, :, cols] = got[2 * q * BLOCK:(2 * q + 1) * BLOCK, :quarter]
+            gb[k, z, x, :, cols] = got[(2 * q + 1) * BLOCK:(2 * q + 2) * BLOCK, :quarter]
+        ga[k, z, x, :, width:] = got[:BLOCK, quarter:]
 
     ag = {}
     halves = (
@@ -327,15 +335,12 @@
             rs[k, h, 7].wait_recv()
             value = part[(k, z, x, slice(None), cols_of(h, None))].astype(F32)
             value += t2[k, h, 0].astype(F32) + t2[k, h, 1].astype(F32)
-            fin[:, cols_of(h, None)] = value.astype(BF16)
-        row = iota((slots, BLOCK), 0)
-        inner = row % BLOCK
-        home = iota((slots, BLOCK), 1) == (row // BLOCK) * PAIR + inner % PAIR
-        total = jnp.zeros((slots, eighth), F32)
-        for q in range(8):
-            total += dot(select(home & (inner // PAIR == q)), fin[:, q * eighth:(q + 1) * eighth])
-        rsnd[k, :, :, :eighth] = total.astype(BF16).reshape(OWNERS, BLOCK, eighth)
+            for q in range(4):
+                at = (4 * h + q) * BLOCK
+                fin[at:at + BLOCK, :eighth] = value[:, q * eighth:(q + 1) * eighth].astype(BF16)
         span = pl.ds(0, eighth)
+        if k == 0:
+            fin[CHUNKS * BLOCK:, eighth:] = jnp.zeros((slots - CHUNKS * BLOCK, LANES), BF16)
         if k == CHUNKS - 1:
             span = pl.ds(0, eighth + LANES)
             for d in range(1, SIDE * SIDE):
@@ -349,18 +354,19 @@
                 axis=1, keepdims=True,
             )
             column = jnp.broadcast_to(column, (held, LANES)).astype(BF16)
-            row = iota((slots, held), 0)
-            inner = row % BLOCK
-            place = (inner // PAIR) * BLOCK + (row // BLOCK) * PAIR + inner % PAIR
-            probs = dot(select(iota((slots, held), 1) == place), column)
-            rsnd[k, :, :, eighth:] = probs.astype(BF16).reshape(OWNERS, BLOCK, LANES)
+            fin[:held, eighth:] = column
+        row, col = iota((slots, slots), 0), iota((slots, slots), 1)
+        inner = row % BLOCK
+        place = (inner // PAIR) * BLOCK + (row // BLOCK) * PAIR + inner % PAIR
+        moved = dot(select(col == place), fin[:, span]).astype(BF16)
+        rsnd[k, :, :, span] = moved.reshape(OWNERS, BLOCK, moved.shape[1])
         for dc in range(1, OWNERS):
             to = (c + dc) % OWNERS
             rt[k, dc] = send(
                 rsnd.at[k, to, :, span], rrcv.at[k, c, :, span],
                 rt_send.at[k, dc], rt_recv.at[k, dc], {"ctx": to, "tp": t},
             )
-        rrcv[k, c] = rsnd[k, c]
+        rrcv[k, c, :, span] = rsnd[k, c, :, span]
 
     pp = {}
 
@@ -385,13 +391,8 @@
             rows_grad = gb[:, :, :, :, at].reshape(CHUNKS * ROWS, wide)
             wd[:, at] = dot_tn(wei[...], rows_grad).astype(BF16)
 
-    stores = [
-        pltpu.make_async_copy(src, dst, o_sem.at[i])
-        for i, (src, dst) in enumerate(
-            ((wg, out_wg.at[0]), (wu, out_wu.at[0]), (wd, out_wd.at[0]))
-        )
-    ]
-
+    for copy in stacking:
+        copy.wait()
     build(0)
     pl.semaphore_wait(barrier, OWNERS - 1 + SIDE * SIDE - 1)
     disperse(0)
@@ -444,41 +445,50 @@
     weight_in(6, 8)
     r4(2)
     weight_in(8, 10)
-    stores[0].start()
-    stores[1].start()
     r5(2)
     weight_down()
-    stores[2].start()
-
+
+    row, col = iota((8 * count, slots), 0), iota((8 * count, slots), 1)
+    inner = col % BLOCK
+    base = (col // BLOCK) * CAPACITY + inner % PAIR
+    here = inner // PAIR == row // count
+    spread = jnp.where(
+        iota((8 * count, count), 0) % count == iota((8 * count, count), 1),
+        jnp.broadcast_to(target_row[:, :count], (8 * count, count)), 0.0,
+    )
+    aimed = jnp.broadcast_to(jnp.sum(spread, axis=1, keepdims=True), (8 * count, slots))
+    total = jnp.zeros((8 * count, eighth), F32)
     for k in range(CHUNKS):
+        hit = select(here & (aimed == (base + PAIR * k).astype(F32)))
         for dc in range(1, OWNERS):
             rt[k, dc].wait_recv()
-    row = iota((count, slots), 1)
-    inner = row % BLOCK
-    base = (row // BLOCK) * CAPACITY + inner % PAIR
-    hits = [
-        jnp.broadcast_to(target, (count, slots)) == (base + PAIR * k).astype(F32)
-        for k in range(CHUNKS)
-    ]
+        total += dot(hit, rrcv[k, :, :, :eighth].reshape(slots, eighth))
     for q in range(8):
-        total = jnp.zeros((count, eighth), F32)
-        for k in range(CHUNKS):
-            total += dot(
-                select(hits[k] & (inner // PAIR == q)),
-                rrcv[k, :, :, :eighth].reshape(slots, eighth),
-            )
-        out_tokens[:, q * eighth:(q + 1) * eighth] = total.astype(BF16)
-    total = jnp.zeros((count, LANES), F32)
-    for k in range(CHUNKS):
-        total += dot(
-            select(hits[k] & (inner // PAIR == k)),
-            rrcv[CHUNKS - 1, :, :, eighth:].reshape(slots, LANES),
+        out_tokens[:, q * eighth:(q + 1) * eighth] = (
+            total[q * count:(q + 1) * count].astype(BF16)
         )
-    out_prob[...] = total.astype(BF16)
+    col = iota((count, slots), 1)
+    inner = col % BLOCK
+    wanted = (col // BLOCK) * CAPACITY + inner
+    hit = (inner < CAPACITY) & (jnp.broadcast_to(target, (count, slots)) == wanted.astype(F32))
+    total = dot(select(hit), rrcv[CHUNKS - 1, :, :, eighth:].reshape(slots, LANES))
+    eye = iota((count, count), 0) == iota((count, count), 1)
+    spread = jnp.where(eye, jnp.broadcast_to(total[:, :1], (count, count)), 0.0)
+    out_prob[...] = jnp.sum(spread, axis=0, keepdims=True).astype(BF16)
 
     for copy in sent:
         copy.wait_send()
-    for copy in stores:
+
+
+def place(*refs):
+    sources, targets, sem = refs[:5], refs[5:10], refs[10]
+    copies = [
+        pltpu.make_async_copy(src, dst, sem.at[i])
+        for i, (src, dst) in enumerate(zip(sources, targets))
+    ]
+    for copy in copies:
+        copy.start()
+    for copy in copies:
         copy.wait()
 
 
@@ -490,21 +500,19 @@
     anywhere = pl.BlockSpec(memory_space=pl.ANY)
     rows = CHUNKS * ROWS
     dma = pltpu.SemaphoreType.DMA
-    grad_tokens, grad_prob, grad_wg, grad_wu, grad_wd = pl.pallas_call(
+    made = pl.pallas_call(
         kernel,
         out_shape=(
-            jax.ShapeDtypeStruct((count, width), BF16),
-            jax.ShapeDtypeStruct((count, LANES), BF16),
-            jax.ShapeDtypeStruct(w_gate.shape, BF16),
-            jax.ShapeDtypeStruct(w_up.shape, BF16),
-            jax.ShapeDtypeStruct(w_down.shape, BF16),
+            pltpu.VMEM((count, width), BF16),
+            pltpu.VMEM((1, count), BF16),
+            pltpu.VMEM(w_gate.shape, BF16),
+            pltpu.VMEM(w_up.shape, BF16),
+            pltpu.VMEM(w_down.shape, BF16),
         ),
-        in_specs=[vmem] * 4 + [anywhere] * 3,
-        out_specs=[vmem] * 2 + [anywhere] * 3,
+        in_specs=[anywhere] * 2 + [vmem] * 2 + [anywhere] * 3,
+        out_specs=[vmem] * 5,
         scratch_shapes=[
-            pltpu.VMEM((width, units), BF16),
-            pltpu.VMEM((width, units), BF16),
-            pltpu.VMEM((units, width), BF16),
+            pltpu.VMEM((8 * count, quarter + LANES), BF16),
             pltpu.VMEM((CHUNKS, OWNERS, BLOCK, quarter + LANES), BF16),
             pltpu.VMEM((CHUNKS, OWNERS, BLOCK, quarter + LANES), BF16),
             pltpu.VMEM((CHUNKS, SIDE, SIDE, BLOCK, width + LANES), BF16),
@@ -514,7 +522,7 @@
             pltpu.VMEM((CHUNKS, 2, 2, SIDE, BLOCK, half), BF16),
             pltpu.VMEM((CHUNKS, 2, 2, BLOCK, quarter), BF16),
             pltpu.VMEM((CHUNKS, 2, 2, BLOCK, half), BF16),
-            pltpu.VMEM((BLOCK, width), BF16),
+            pltpu.VMEM((8 * BLOCK, eighth + LANES), BF16),
             pltpu.VMEM((CHUNKS, OWNERS, BLOCK, eighth + LANES), BF16),
             pltpu.VMEM((CHUNKS, OWNERS, BLOCK, eighth + LANES), BF16),
             pltpu.VMEM((3, ROWS, units), F32),
@@ -522,7 +530,7 @@
             pltpu.VMEM((rows, units), BF16),
             pltpu.VMEM((SIDE, SIDE, 8, LANES), F32),
             pltpu.VMEM((SIDE * SIDE, 8, LANES), F32),
-            dma((3,)),
+            dma((8,)),
             dma((3,)),
             dma((CHUNKS, OWNERS)),
             dma((CHUNKS, OWNERS)),
@@ -536,10 +544,18 @@
             dma((CHUNKS, OWNERS)),
         ],
         compiler_params=pltpu.CompilerParams(
-            collective_id=0, has_side_effects=True, vmem_limit_bytes=60 * 2**20
+            collective_id=0, has_side_effects=True, vmem_limit_bytes=46 * 2**20
         ),
-    )(tokens, grad_out, gate_prob[None], expert_ids, w_gate, w_up, w_down)
-    return grad_tokens, grad_prob[:, 0], grad_wg, grad_wu, grad_wd
+    )(tokens, grad_out, gate_prob[None], expert_ids.reshape(1, count), w_gate, w_up, w_down)
+    grad_tokens, grad_prob, grad_wg, grad_wu, grad_wd = pl.pallas_call(
+        place,
+        out_shape=tuple(jax.ShapeDtypeStruct(part.shape, BF16) for part in made),
+        in_specs=[anywhere] * 5,
+        out_specs=[anywhere] * 5,
+        scratch_shapes=[dma((5,))],
+        compiler_params=pltpu.CompilerParams(vmem_limit_bytes=2**20),
+    )(*made)
+    return grad_tokens, grad_prob[0], grad_wg, grad_wu, grad_wd
 
 
 def solution(mesh):

time: 178 us -> 165 us (0.927)
  local copies, waits for them, and re-layouts: 14.4 us -> 0 us
  Pallas kernels: 162 us -> 164 us
    unnamed x9 -> x0, local copies, waits for them, and re-layouts: 13.1 us -> none
    pallas_call x1 -> x2, Pallas kernels: 162 us -> 164 us  [the longest x1 160 us: per_device(): pl.pallas_call(kernel, out_shape=(pltpu.VMEM((count, width), BF16), pltpu...]
where the time goes in v3:
time: 165 us
  Pallas kernels  164 us (99%)
    pallas_call x1, Pallas kernels, per_device(): pl.pallas_call(kernel, out_shape=(pltpu.VMEM((count, width), BF16), pltpu...  160 us
    pallas_call x1, Pallas kernels, per_device(): pl.pallas_call(place, out_shape=tuple((jax.ShapeDtypeStruct(part.shape, B...  4.56 us

profile of v3, /device:TPU:0, one launch (start us, length us, event | category | flops | bytes accessed | tf_op | source)
XLA Modules:
  0.0 165.2 jit_solution(2320988413529008328)
XLA Ops:
  0.6 159.8 %shard_map.110 = (bf16[32,5120]{1,0:T(8,128)(2,1)S(1)}, bf16[1,32]{1,0:T(2,128)(2,1)S(1)}, bf16[1,5120,384]{2,1,0:T(8,128)(2,1)S(1)}, bf16[1,5120,384]{2,1,0:T(8,128)(2,1)S(1)}, bf16[1,384,5120]{2,1,0:T(8,128)(2,1)S(1)}) custom-call(bf16[32,5120]{1,0:T(8,128)(2,1)} %tokens.1, bf16[32,5120]{1,0:T(8,128)(2,1)} %grads.1, bf16[1,32]{1,0:T(2,128)(2,1)} %bitcast.3, ...), custom_call_target="tpu_custom_call" | custom-call | tf_op jit(solution)/shard_map/pallas_call | solution.py:503
  160.5 4.6 %shard_map.111 = (bf16[32,5120]{1,0:T(8,128)(2,1)}, bf16[1,32]{1,0:T(2,128)(2,1)}, bf16[1,5120,384]{2,1,0:T(8,128)(2,1)}, bf16[1,5120,384]{2,1,0:T(8,128)(2,1)}, bf16[1,384,5120]{2,1,0:T(8,128)(2,1)}) custom-call(bf16[32,5120]{1,0:T(8,128)(2,1)S(1)} %get-tuple-element.15.refs_0_, bf16[1,32]{1,0:T(2,128)(2,1)S(1)} %get-tuple-element.16.refs_1_, ...), custom_call_target="tpu_custom_call" | custom-call | tf_op jit(solution)/shard_map/pallas_call | solution.py:550

commit v4 on v3

v4 whole, which is shorter than its diff:
```python
import jax
import jax.numpy as jnp
from jax import lax
from jax.experimental import pallas as pl
from jax.experimental.pallas import tpu as pltpu
from jax.sharding import PartitionSpec as P

F32 = jnp.float32
BF16 = jnp.bfloat16
SIDE = 4
OWNERS = 8
PAIR = 2
CHUNKS = 3
CAPACITY = PAIR * CHUNKS
BLOCK = OWNERS * PAIR
ROWS = SIDE * SIDE * BLOCK
LANES = 128


def dot(a, b):
    return jnp.dot(a, b, preferred_element_type=F32)


def dot_nt(a, b):
    return lax.dot_general(a, b, (((1,), (1,)), ((), ())), preferred_element_type=F32)


def dot_tn(a, b):
    return lax.dot_general(a, b, (((0,), (0,)), ((), ())), preferred_element_type=F32)


def iota(shape, dim):
    return lax.broadcasted_iota(jnp.int32, shape, dim)


def select(mask):
    return jnp.where(mask, 1.0, 0.0).astype(BF16)


def column(line):
    count = line.shape[1]
    eye = iota((count, count), 0) == iota((count, count), 1)
    spread = jnp.broadcast_to(line[...].astype(F32), (count, count))
    return jnp.sum(jnp.where(eye, spread, 0.0), axis=1, keepdims=True)


def targets(ids):
    count = ids.shape[1]
    chosen = column(ids)
    onehot = jnp.where(chosen == iota((count, LANES), 1).astype(F32), 1.0, 0.0)
    lower = select(iota((count, count), 0) >= iota((count, count), 1))
    ranks = dot(lower, onehot.astype(BF16))
    slot = jnp.sum(ranks * onehot, axis=1, keepdims=True) - 1.0
    return chosen * CAPACITY + slot


def kernel(
    tokens, grads, prob, ids, wg_in, wu_in, wd_in,
    rrcv, out_wg, out_wu, out_wd,
    stk, snd, rcv, ga, gb, part, s1, s2, t1, t2, fin, rsnd,
    acc, dd, wei, pps, ppr,
    i_sem, w_sem, p1_send, p1_recv, ag_send, ag_recv, rs_send, rs_recv,
    pp_send, pp_recv, rt_send, rt_recv,
):
    count, width = tokens.shape
    wg, wu, wd = out_wg.at[0], out_wu.at[0], out_wd.at[0]
    units = wg.shape[1]
    quarter, eighth, half = width // 4, width // 8, width // 2
    c = lax.axis_index("ctx")
    t = lax.axis_index("tp")
    x, z = t // SIDE, t % SIDE

    def at_xz(xd, zd):
        return {"ctx": c, "tp": xd * SIDE + zd}

    def step(p, by):
        return (p + by + SIDE) % SIDE

    barrier = pltpu.get_barrier_semaphore()
    for dc in range(1, OWNERS):
        pl.semaphore_signal(
            barrier, inc=1, device_id={"ctx": (c + dc) % OWNERS, "tp": t},
            device_id_type=pl.DeviceIdType.MESH,
        )
    for d in range(1, SIDE * SIDE):
        pl.semaphore_signal(
            barrier, inc=1, device_id=at_xz(step(x, d // SIDE), step(z, d % SIDE)),
            device_id_type=pl.DeviceIdType.MESH,
        )

    stacking = [
        pltpu.make_async_copy(
            src.at[:, q * quarter:(q + 1) * quarter],
            stk.at[pl.ds((2 * q + n) * count, count), pl.ds(0, quarter)],
            i_sem.at[2 * q + n],
        )
        for q in range(4)
        for n, src in enumerate((tokens, grads))
    ]
    for copy in stacking:
        copy.start()
    loads = [
        pltpu.make_async_copy(src, dst, w_sem.at[i])
        for i, (src, dst) in enumerate(((wg_in.at[0], wg), (wu_in.at[0], wu), (wd_in.at[0], wd)))
    ]
    for copy in loads:
        copy.start()

    sent = []

    def drain(keep=0):
        while len(sent) > keep:
            sent.pop(0).wait_send()

    def send(src, dst, send_sem, recv_sem, device):
        copy = pltpu.make_async_remote_copy(
            src_ref=src, dst_ref=dst, send_sem=send_sem, recv_sem=recv_sem,
            device_id=device, device_id_type=pl.DeviceIdType.MESH,
        )
        copy.start()
        sent.append(copy)
        return copy

    deck = 8 * count

    target = targets(ids)
    target_row = jnp.sum(
        jnp.where(
            iota((count, deck), 0) == iota((count, deck), 1) % count,
            jnp.broadcast_to(target, (count, deck)), 0.0,
        ),
        axis=0, keepdims=True,
    )
    stk[:, quarter:] = jnp.zeros((deck, LANES), BF16)
    stk[:count, quarter:] = jnp.broadcast_to(column(prob), (count, LANES)).astype(BF16)
    slots = OWNERS * BLOCK

    def build(k):
        row, col = iota((slots, deck), 0), iota((slots, deck), 1)
        inner = row % BLOCK
        want = (row // BLOCK) * CAPACITY + PAIR * k + inner % PAIR
        hit = jnp.broadcast_to(target_row, (slots, deck)) == want.astype(F32)
        pick = select(hit & (inner // PAIR == col // count))
        snd[k] = dot(pick, stk[...]).astype(BF16).reshape(OWNERS, BLOCK, quarter + LANES)

    p1 = {}

    def disperse(k):
        for dc in range(1, OWNERS):
            to = (c + dc) % OWNERS
            p1[k, dc] = send(
                snd.at[k, to], rcv.at[k, c], p1_send.at[k, dc], p1_recv.at[k, dc],
                {"ctx": to, "tp": t},
            )
        rcv[k, c] = snd[k, c]

    def assemble(k):
        for dc in range(1, OWNERS):
            p1[k, dc].wait_recv()
        row, col = iota((slots, slots), 0), iota((slots, slots), 1)
        one = row % BLOCK
        where = (one // PAIR) * BLOCK + (row // BLOCK) * PAIR + one % PAIR
        got = dot(select(col == where), rcv[k].reshape(slots, quarter + LANES)).astype(BF16)
        for q in range(4):
            cols = slice(q * quarter, (q + 1) * quarter)
            ga[k, z, x, :, cols] = got[2 * q * BLOCK:(2 * q + 1) * BLOCK, :quarter]
            gb[k, z, x, :, cols] = got[(2 * q + 1) * BLOCK:(2 * q + 2) * BLOCK, :quarter]
        ga[k, z, x, :, width:] = got[:BLOCK, quarter:]

    ag = {}
    halves = (
        (pl.ds(0, half), pl.ds(half, half + LANES)),
        (pl.ds(0, half), pl.ds(half, half)),
    )

    def ag_send_one(k, arr, n, ref, device):
        ag[k, arr, n] = send(ref, ref, ag_send.at[k, arr, n], ag_recv.at[k, arr, n], device)

    def near(arr, stage, by):
        along_x = (arr == 0) == (stage == 1)
        return at_xz(step(x, by), z) if along_x else at_xz(x, step(z, by))

    BOTH = ((0, 1), (1, -1))
    AROUND = (0, -1, 1, 2)

    def block(k, arr, first, second, cols=None):
        xd, zd = (step(x, first), step(z, second)) if arr == 0 else (step(x, second), step(z, first))
        buf = (ga, gb)[arr]
        return buf.at[k, zd, xd] if cols is None else buf.at[k, zd, xd, :, cols]

    def across(k, arr, n):
        for side, by in ((0, 1), (1, -1)):
            ag_send_one(k, arr, 4 + 2 * n + side, block(k, arr, AROUND[n], 0), near(arr, 2, by))

    def g1(k):
        for arr in range(2):
            ag_send_one(k, arr, 0, block(k, arr, 0, 0), near(arr, 1, 1))
            ag_send_one(k, arr, 1, block(k, arr, 0, 0), near(arr, 1, -1))
        for arr in range(2):
            across(k, arr, 0)

    def g2(k, arr, side):
        by = BOTH[side][1]
        ag[k, arr, side].wait_recv()
        ag_send_one(k, arr, 2 + side, block(k, arr, -by, 0, halves[arr][side]), near(arr, 1, by))
        across(k, arr, 1 + side)

    def g3(k, arr):
        ag[k, arr, 2].wait_recv()
        ag[k, arr, 3].wait_recv()
        across(k, arr, 3)

    def g4(k, arr, n, side):
        by = BOTH[side][1]
        ag[k, arr, 4 + 2 * n + side].wait_recv()
        ag_send_one(
            k, arr, 12 + 2 * n + side,
            block(k, arr, AROUND[n], -by, halves[arr][side]), near(arr, 2, by),
        )

    def g5(k):
        for arr in range(2):
            for n in range(12, 20):
                ag[k, arr, n].wait_recv()

    deep = quarter
    wide = width // 10

    def products(k, first, last):
        def one(i, fresh):
            at = pl.ds(pl.multiple_of(i * deep, deep), deep)
            rows_in = ga[k, :, :, :, at].reshape(ROWS, deep)
            rows_grad = gb[k, :, :, :, at].reshape(ROWS, deep)
            gu = dot(rows_in, jnp.concatenate([wg[at, :], wu[at, :]], axis=1))
            raw = dot_nt(rows_grad, wd[:, at])
            acc[:, :2 * units] = gu if fresh else acc[:, :2 * units] + gu
            acc[:, 2 * units:] = raw if fresh else acc[:, 2 * units:] + raw

        if first == 0:
            one(0, True)
            first = 1

        @pl.loop(first, last)
        def _(i):
            one(i, False)

    def forward(k):
        part_rows = 2 * LANES // 4

        @pl.loop(0, ROWS // part_rows)
        def _(i):
            at = pl.ds(pl.multiple_of(i * part_rows, part_rows), part_rows)
            keep = pl.ds(pl.multiple_of(k * ROWS + i * part_rows, part_rows), part_rows)
            g, u, raw = acc[at, :units], acc[at, units:2 * units], acc[at, 2 * units:]
            sig = jax.nn.sigmoid(g)
            act = g * sig
            hidden = act * u
            probs = ga[k, i, :, :, width:].reshape(part_rows, LANES).astype(F32)[:, :1]
            wei[keep, :] = (probs * hidden).astype(BF16)
            dh = probs * raw
            dd[keep, :units] = (dh * u * sig * (1.0 + g * (1.0 - sig))).astype(BF16)
            dd[keep, units:] = (dh * act).astype(BF16)
            sums = jnp.broadcast_to(
                jnp.sum(hidden * raw, axis=1, keepdims=True), (part_rows, LANES)
            )
            spot = iota((part_rows, LANES), 1) == k * BLOCK + iota((part_rows, LANES), 0) % BLOCK
            lanes = jnp.sum(
                jnp.where(spot, sums, 0.0).reshape(SIDE, BLOCK, LANES), axis=1, keepdims=True
            )
            lanes = jnp.broadcast_to(lanes, (SIDE, 8, LANES))
            pps[i] = lanes if k == 0 else pps[i] + lanes

    def backward(k, p, h):
        rows = dd[k * ROWS:(k + 1) * ROWS, :]

        if True:
            at = pl.ds(h * half + p * quarter, quarter)
            value = dot_nt(rows, jnp.concatenate([wg[at, :], wu[at, :]], axis=1))
            part[k, :, :, :, at] = value.astype(BF16).reshape(SIDE, SIDE, BLOCK, quarter)

    rs = {}

    def rs_send_one(k, h, p, n, src, dst, device):
        m = 2 * h + p
        rs[k, m, n] = send(src, dst, rs_send.at[k, m, n], rs_recv.at[k, m, n], device)

    def cols_of(h, p, side=None):
        at = h * half + p * quarter
        return slice(at, at + quarter) if side is None else slice(at + side * eighth, at + (side + 1) * eighth)

    def group(h, by):
        return (step(z, by), slice(None)) if h == 0 else (slice(None), step(x, by))

    def own(h, by):
        return (z, step(x, by)) if h == 0 else (step(z, by), x)

    def add_into(where, others):
        value = part[where].astype(F32)
        for other in others:
            value += other[...].astype(F32)
        part[where] = value.astype(BF16)

    def r1(k, p, h):
        far = (k,) + group(h, 2) + (slice(None),)
        for side, by in BOTH:
            rs_send_one(k, h, p, side, part.at[far + (cols_of(h, p, side),)],
                        s1.at[k, 2 * h + p, side], near(h, 2, by))

    def r2(k, p, h, side):
        by = BOTH[side][1]
        rs[k, 2 * h + p, side].wait_recv()
        to = (k,) + group(h, by) + (slice(None),)
        add_into(to + (cols_of(h, p, side),), (s1.at[k, 2 * h + p, side],))
        rs_send_one(k, h, p, 2 + side, part.at[to + (cols_of(h, p),)],
                    s2.at[k, 2 * h + p, side], near(h, 2, by))

    def r3(k, p, h):
        m = 2 * h + p
        rs[k, m, 2].wait_recv()
        rs[k, m, 3].wait_recv()
        far = (k,) + own(h, 2) + (slice(None),)
        mine = (k,) + group(h, 0) + (slice(None), cols_of(h, p))
        add_into(mine, (s2.at[k, m, 0], s2.at[k, m, 1]))
        for side, by in BOTH:
            rs_send_one(k, h, p, 4 + side, part.at[far + (cols_of(h, p, side),)],
                        t1.at[k, m, side], near(h, 1, by))

    def r4(k, p, h, side):
        m = 2 * h + p
        by = BOTH[side][1]
        rs[k, m, 4 + side].wait_recv()
        to = (k,) + own(h, by) + (slice(None),)
        add_into(to + (cols_of(h, p, side),), (t1.at[k, m, side],))
        rs_send_one(k, h, p, 6 + side, part.at[to + (cols_of(h, p),)],
                    t2.at[k, m, side], near(h, 1, by))

    rt = {}

    def r5(k):
        for m in range(4):
            rs[k, m, 6].wait_recv()
            rs[k, m, 7].wait_recv()
            value = part[(k, z, x, slice(None), cols_of(m // 2, m % 2))].astype(F32)
            value += t2[k, m, 0].astype(F32) + t2[k, m, 1].astype(F32)
            for q in range(2):
                at = (2 * m + q) * BLOCK
                fin[at:at + BLOCK, :eighth] = value[:, q * eighth:(q + 1) * eighth].astype(BF16)
        span = pl.ds(0, eighth)
        if k == 0:
            fin[CHUNKS * BLOCK:, eighth:] = jnp.zeros((slots - CHUNKS * BLOCK, LANES), BF16)
        if k == CHUNKS - 1:
            span = pl.ds(0, eighth + LANES)
            for d in range(1, SIDE * SIDE):
                pp[d].wait_recv()
            ppr[0] = pps[z, x]
            summed = jnp.sum(ppr[...], axis=0)[:1]
            held = CHUNKS * BLOCK
            diagonal = iota((held, LANES), 0) == iota((held, LANES), 1)
            column = jnp.sum(
                jnp.where(diagonal, jnp.broadcast_to(summed, (held, LANES)), 0.0),
                axis=1, keepdims=True,
            )
            column = jnp.broadcast_to(column, (held, LANES)).astype(BF16)
            fin[:held, eighth:] = column
        row, col = iota((slots, slots), 0), iota((slots, slots), 1)
        inner = row % BLOCK
        place = (inner // PAIR) * BLOCK + (row // BLOCK) * PAIR + inner % PAIR
        moved = dot(select(col == place), fin[:, span]).astype(BF16)
        rsnd[k, :, :, span] = moved.reshape(OWNERS, BLOCK, moved.shape[1])
        for dc in range(1, OWNERS):
            to = (c + dc) % OWNERS
            rt[k, dc] = send(
                rsnd.at[k, to, :, span], rrcv.at[k, c, :, span],
                rt_send.at[k, dc], rt_recv.at[k, dc], {"ctx": to, "tp": t},
            )
        rrcv[k, c, :, span] = rsnd[k, c, :, span]

    pp = {}

    def probs_out():
        for d in range(1, SIDE * SIDE):
            xd, zd = step(x, d // SIDE), step(z, d % SIDE)
            pp[d] = send(pps.at[zd, xd], ppr.at[d], pp_send.at[d], pp_recv.at[d], at_xz(xd, zd))

    def weight_in(first, last):
        @pl.loop(first, last)
        def _(i):
            at = pl.ds(pl.multiple_of(i * wide, wide), wide)
            rows_in = ga[:, :, :, :, at].reshape(CHUNKS * ROWS, wide)
            value = dot_tn(rows_in, dd[...])
            wg[at, :] = value[:, :units].astype(BF16)
            wu[at, :] = value[:, units:].astype(BF16)

    def weight_down(first, last):
        @pl.loop(first, last)
        def _(i):
            at = pl.ds(pl.multiple_of(i * wide, wide), wide)
            rows_grad = gb[:, :, :, :, at].reshape(CHUNKS * ROWS, wide)
            wd[:, at] = dot_tn(wei[...], rows_grad).astype(BF16)

    for copy in stacking:
        copy.wait()
    build(0)
    pl.semaphore_wait(barrier, OWNERS - 1 + SIDE * SIDE - 1)
    disperse(0)
    build(1)
    build(2)
    assemble(0)
    g1(0)
    disperse(1)
    g2(0,0,0)
    g2(0,0,1)
    g2(0,1,0)
    g2(0,1,1)
    g4(0,1,0,0)
    g4(0,1,0,1)
    g4(0,0,0,0)
    g4(0,0,0,1)
    g3(0,0)
    g4(0,0,1,0)
    g4(0,0,1,1)
    g4(0,1,1,0)
    g4(0,1,1,1)
    assemble(1)
    g1(1)
    disperse(2)
    g4(0,0,2,0)
    g4(0,0,2,1)
    g4(0,1,2,0)
    g4(0,1,2,1)
    g3(0,1)
    g4(0,0,3,0)
    g4(0,0,3,1)
    g2(1,0,0)
    g2(1,0,1)
    g4(1,1,0,0)
    g4(1,1,0,1)
    g2(1,1,0)
    g2(1,1,1)
    g4(1,0,0,0)
    g4(1,0,0,1)
    g4(0,1,3,0)
    g4(0,1,3,1)
    g3(1,0)
    g4(1,0,1,0)
    g4(1,0,1,1)
    g4(1,1,1,0)
    g4(1,1,1,1)
    assemble(2)
    g1(2)
    g4(1,0,2,0)
    g4(1,0,2,1)
    g4(1,1,2,0)
    g4(1,1,2,1)
    g3(1,1)
    g5(0)
    for copy in loads:
        copy.wait()
    products(0,0,3)
    g4(1,0,3,0)
    products(0,3,4)
    g4(1,0,3,1)
    g2(2,0,0)
    g2(2,0,1)
    forward(0)
    backward(0,0,0)
    backward(0,0,1)
    backward(0,1,0)
    g4(2,1,0,0)
    backward(0,1,1)
    g2(2,1,0)
    g4(2,1,0,1)
    g2(2,1,1)
    g4(2,0,0,0)
    g4(2,0,0,1)
    g4(1,1,3,0)
    g4(1,1,3,1)
    g3(2,0)
    g4(2,1,1,1)
    g4(2,0,1,0)
    g4(2,0,1,1)
    g4(2,1,1,0)
    g4(2,0,2,0)
    g4(2,0,2,1)
    g4(2,1,2,0)
    g4(2,1,2,1)
    g3(2,1)
    g5(1)
    r1(0,0,0)
    r1(0,0,1)
    r1(0,1,0)
    r1(0,1,1)
    products(1,0,3)
    g4(2,0,3,0)
    products(1,3,4)
    g4(2,0,3,1)
    forward(1)
    g4(2,1,3,0)
    backward(1,0,0)
    g4(2,1,3,1)
    backward(1,0,1)
    backward(1,1,0)
    r2(0,0,1,0)
    r2(0,0,1,1)
    r2(0,0,0,0)
    backward(1,1,1)
    r2(0,1,1,0)
    r2(0,0,0,1)
    r2(0,1,1,1)
    r2(0,1,0,0)
    r2(0,1,0,1)
    g5(2)
    r1(1,0,0)
    r1(1,0,1)
    r1(1,1,0)
    r1(1,1,1)
    products(2,0,1)
    r3(0,0,1)
    products(2,1,2)
    r3(0,0,0)
    products(2,2,3)
    r3(0,1,1)
    products(2,3,4)
    r3(0,1,0)
    r2(1,0,0,0)
    r2(1,0,1,0)
    r2(1,0,1,1)
    forward(2)
    r4(0,0,0,0)
    r4(0,0,0,1)
    r2(1,0,0,1)
    r2(1,1,0,0)
    r2(1,1,1,0)
    r4(0,0,1,0)
    r2(1,1,1,1)
    r4(0,1,0,0)
    r4(0,1,0,1)
    r4(0,1,1,0)
    r2(1,1,0,1)
    r4(0,0,1,1)
    backward(2,0,0)
    r4(0,1,1,1)
    r1(2,0,0)
    backward(2,0,1)
    r1(2,0,1)
    backward(2,1,0)
    r1(2,1,0)
    backward(2,1,1)
    r3(1,0,1)
    r1(2,1,1)
    probs_out()
    r3(1,0,0)
    weight_in(0,3)
    r3(1,1,0)
    r3(1,1,1)
    weight_in(3,4)
    r2(2,0,0,0)
    r2(2,0,1,0)
    r2(2,0,1,1)
    r5(0)
    r4(1,0,0,0)
    r4(1,0,0,1)
    r4(1,0,1,0)
    r4(1,1,0,0)
    r4(1,1,0,1)
    r4(1,1,1,0)
    r2(2,0,0,1)
    r2(2,1,0,0)
    r2(2,1,0,1)
    r4(1,0,1,1)
    r2(2,1,1,0)
    r2(2,1,1,1)
    r4(1,1,1,1)
    weight_in(4,7)
    r3(2,0,1)
    weight_in(7,9)
    r3(2,0,0)
    weight_in(9,10)
    weight_down(0,2)
    r4(2,0,1,0)
    r3(2,1,1)
    r3(2,1,0)
    r4(2,0,0,0)
    r4(2,0,0,1)
    weight_down(2,4)
    r5(1)
    r4(2,0,1,1)
    r4(2,1,0,0)
    r4(2,1,0,1)
    r4(2,1,1,0)
    r4(2,1,1,1)
    weight_down(4,10)
    r5(2)

    for k in range(CHUNKS):
        for dc in range(1, OWNERS):
            rt[k, dc].wait_recv()
    drain()


def finish(
    ids, back_in, wg, wu, wd, tokens_out, out_prob, out_wg, out_wu, out_wd,
    back, out_tokens, sem,
):
    copies = [
        pltpu.make_async_copy(src, dst, sem.at[i])
        for i, (src, dst) in enumerate(
            ((back_in, back), (wg, out_wg), (wu, out_wu), (wd, out_wd))
        )
    ]
    for copy in copies:
        copy.start()
    count = ids.shape[1]
    eighth = back.shape[3] - LANES
    slots = OWNERS * BLOCK
    target = targets(ids)
    aimed = jnp.broadcast_to(jnp.concatenate([target] * 8, axis=0), (8 * count, slots))
    row, col = iota((8 * count, slots), 0), iota((8 * count, slots), 1)
    inner = col % BLOCK
    base = (col // BLOCK) * CAPACITY + inner % PAIR
    here = inner // PAIR == row // count
    copies.pop(0).wait()
    total = jnp.zeros((8 * count, eighth), F32)
    for k in range(CHUNKS):
        hit = select(here & (aimed == (base + PAIR * k).astype(F32)))
        total += dot(hit, back[k, :, :, :eighth].reshape(slots, eighth))
    for q in range(8):
        out_tokens[:, q * eighth:(q + 1) * eighth] = (
            total[q * count:(q + 1) * count].astype(BF16)
        )
    copies.append(pltpu.make_async_copy(out_tokens, tokens_out, sem.at[4]))
    copies[-1].start()
    col = iota((count, slots), 1)
    inner = col % BLOCK
    wanted = (col // BLOCK) * CAPACITY + inner
    hit = (inner < CAPACITY) & (jnp.broadcast_to(target, (count, slots)) == wanted.astype(F32))
    total = dot(select(hit), back[CHUNKS - 1, :, :, eighth:].reshape(slots, LANES))
    eye = iota((count, count), 0) == iota((count, count), 1)
    spread = jnp.where(eye, jnp.broadcast_to(total[:, :1], (count, count)), 0.0)
    out_prob[...] = jnp.sum(spread, axis=0, keepdims=True).astype(BF16)
    for copy in copies:
        copy.wait()


def per_device(tokens, grad_out, gate_prob, expert_ids, w_gate, w_up, w_down):
    count, width = tokens.shape
    units = w_gate.shape[2]
    quarter, eighth, half = width // 4, width // 8, width // 2
    vmem = pl.BlockSpec(memory_space=pltpu.VMEM)
    anywhere = pl.BlockSpec(memory_space=pl.ANY)
    rows = CHUNKS * ROWS
    dma = pltpu.SemaphoreType.DMA
    ids = expert_ids.reshape(1, count)
    back, *made = pl.pallas_call(
        kernel,
        out_shape=(
            pltpu.VMEM((CHUNKS, OWNERS, BLOCK, eighth + LANES), BF16),
            pltpu.VMEM(w_gate.shape, BF16),
            pltpu.VMEM(w_up.shape, BF16),
            pltpu.VMEM(w_down.shape, BF16),
        ),
        in_specs=[anywhere] * 2 + [vmem] * 2 + [anywhere] * 3,
        out_specs=[vmem] * 4,
        scratch_shapes=[
            pltpu.VMEM((8 * count, quarter + LANES), BF16),
            pltpu.VMEM((CHUNKS, OWNERS, BLOCK, quarter + LANES), BF16),
            pltpu.VMEM((CHUNKS, OWNERS, BLOCK, quarter + LANES), BF16),
            pltpu.VMEM((CHUNKS, SIDE, SIDE, BLOCK, width + LANES), BF16),
            pltpu.VMEM((CHUNKS, SIDE, SIDE, BLOCK, width), BF16),
            pltpu.VMEM((CHUNKS, SIDE, SIDE, BLOCK, width), BF16),
            pltpu.VMEM((CHUNKS, 4, 2, SIDE, BLOCK, eighth), BF16),
            pltpu.VMEM((CHUNKS, 4, 2, SIDE, BLOCK, quarter), BF16),
            pltpu.VMEM((CHUNKS, 4, 2, BLOCK, eighth), BF16),
            pltpu.VMEM((CHUNKS, 4, 2, BLOCK, quarter), BF16),
            pltpu.VMEM((8 * BLOCK, eighth + LANES), BF16),
            pltpu.VMEM((CHUNKS, OWNERS, BLOCK, eighth + LANES), BF16),
            pltpu.VMEM((ROWS, 3 * units), F32),
            pltpu.VMEM((rows, 2 * units), BF16),
            pltpu.VMEM((rows, units), BF16),
            pltpu.VMEM((SIDE, SIDE, 8, LANES), F32),
            pltpu.VMEM((SIDE * SIDE, 8, LANES), F32),
            dma((8,)),
            dma((3,)),
            dma((CHUNKS, OWNERS)),
            dma((CHUNKS, OWNERS)),
            dma((CHUNKS, 2, 20)),
            dma((CHUNKS, 2, 20)),
            dma((CHUNKS, 4, 8)),
            dma((CHUNKS, 4, 8)),
            dma((SIDE * SIDE,)),
            dma((SIDE * SIDE,)),
            dma((CHUNKS, OWNERS)),
            dma((CHUNKS, OWNERS)),
        ],
        compiler_params=pltpu.CompilerParams(
            collective_id=0, has_side_effects=True, vmem_limit_bytes=46 * 2**20
        ),
    )(tokens, grad_out, gate_prob[None], ids, w_gate, w_up, w_down)
    grad_tokens, grad_prob, *grads = pl.pallas_call(
        finish,
        out_shape=(
            jax.ShapeDtypeStruct((count, width), BF16),
            jax.ShapeDtypeStruct((1, count), BF16),
            *(jax.ShapeDtypeStruct(grad.shape, BF16) for grad in made),
        ),
        in_specs=[vmem] + [anywhere] * 4,
        out_specs=[anywhere, vmem] + [anywhere] * 3,
        scratch_shapes=[
            pltpu.VMEM(back.shape, BF16), pltpu.VMEM((count, width), BF16), dma((5,))
        ],
        compiler_params=pltpu.CompilerParams(vmem_limit_bytes=6 * 2**20),
    )(ids, back, *made)
    return (grad_tokens, grad_prob[0], *grads)


def solution(mesh):
    in_specs = (
        P(("ctx", "tp"), None),
        P(("ctx", "tp"), None),
        P(("ctx", "tp")),
        P(("ctx", "tp"), None),
        P("ctx", None, "tp"),
        P("ctx", None, "tp"),
        P("ctx", "tp", None),
    )
    out_specs = (
        P(("ctx", "tp"), None),
        P(("ctx", "tp")),
        P("ctx", None, "tp"),
        P("ctx", None, "tp"),
        P("ctx", "tp", None),
    )
    return jax.shard_map(
        per_device, mesh=mesh, in_specs=in_specs, out_specs=out_specs, check_vma=False
    )
```

time: 165 us -> 160 us (0.970)
  Pallas kernels: 164 us -> 158 us
    pallas_call x2, Pallas kernels: 164 us -> 158 us  [the longest x1 153 us: per_device(): pl.pallas_call(kernel, out_shape=(pltpu.VMEM((CHUNKS, OWNERS, BLOCK, eigh...]
where the time goes in v4:
time: 160 us; the launch traced here: 159 us
  Pallas kernels  158 us (99%)
    pallas_call x1, Pallas kernels, per_device(): pl.pallas_call(kernel, out_shape=(pltpu.VMEM((CHUNKS, OWNERS, BLOCK, eigh...  153 us
    pallas_call x1, Pallas kernels, per_device(): pl.pallas_call(finish, out_shape=(jax.ShapeDtypeStruct((count, width), BF...  5.19 us

profile of v4, /device:TPU:0, one launch (start us, length us, event | category | flops | bytes accessed | tf_op | source)
XLA Modules:
  0.0 158.9 jit_solution(14928948289198889163)
XLA Ops:
  0.6 0.0 copy-start
  0.6 152.8 %shard_map.110 = (bf16[3,8,16,768]{3,2,1,0:T(8,128)(2,1)S(1)}, bf16[1,5120,384]{2,1,0:T(8,128)(2,1)S(1)}, bf16[1,5120,384]{2,1,0:T(8,128)(2,1)S(1)}, bf16[1,384,5120]{2,1,0:T(8,128)(2,1)S(1)}) custom-call(bf16[32,5120]{1,0:T(8,128)(2,1)} %tokens.1, bf16[32,5120]{1,0:T(8,128)(2,1)} %grads.1, bf16[1,32]{1,0:T(2,128)(2,1)} %bitcast.5, s32[1,32]{1,0:T(1,128)} %bitcast.3, ...), custom_call_target="tpu_custom_call" | custom-call | tf_op jit(solution)/shard_map/pallas_call | solution.py:654
  153.5 0.0 copy-done
  153.5 5.2 %shard_map.111 = (bf16[32,5120]{1,0:T(8,128)(2,1)}, bf16[1,32]{1,0:T(2,128)(2,1)}, bf16[1,5120,384]{2,1,0:T(8,128)(2,1)}, bf16[1,5120,384]{2,1,0:T(8,128)(2,1)}, bf16[1,384,5120]{2,1,0:T(8,128)(2,1)}) custom-call(s32[1,32]{1,0:T(1,128)S(1)} %bitcast.4, bf16[3,8,16,768]{3,2,1,0:T(8,128)(2,1)S(1)} %get-tuple-element.14.back_in, ...), custom_call_target="tpu_custom_call" | custom-call | tf_op jit(solution)/shard_map/pallas_call | solution.py:699
Async XLA Ops:
  0.6 152.9 %copy-start = (s32[32,1]{0,1:T(1,128)S(1)}, s32[32,1]{0,1:T(1,128)}, u32[]{:S(2)}) copy-start(s32[32,1]{0,1:T(1,128)} %param.10) | copy-start | bytes 388

commit v5 on v4

--- a/solution.py
+++ b/solution.py
@@ -57,7 +57,7 @@
 def kernel(
     tokens, grads, prob, ids, wg_in, wu_in, wd_in,
     rrcv, out_wg, out_wu, out_wd,
-    stk, snd, rcv, ga, gb, part, s1, s2, t1, t2, fin, rsnd,
+    stk, snd, rcv, ga, gb, part, s1, s2, t1, t2, t3, fin, rsnd,
     acc, dd, wei, pps, ppr,
     i_sem, w_sem, p1_send, p1_recv, ag_send, ag_recv, rs_send, rs_recv,
     pp_send, pp_recv, rt_send, rt_recv,
@@ -321,6 +321,11 @@
         far = (k,) + own(h, 2) + (slice(None),)
         mine = (k,) + group(h, 0) + (slice(None), cols_of(h, p))
         add_into(mine, (s2.at[k, m, 0], s2.at[k, m, 1]))
+        if k == CHUNKS - 1:
+            for n, by, dst in ((6, 1, t2.at[k, m, 0]), (7, -1, t2.at[k, m, 1]), (4, 2, t3.at[m])):
+                to = (k,) + own(h, by) + (slice(None), cols_of(h, p))
+                rs_send_one(k, h, p, n, part.at[to], dst, near(h, 1, by))
+            return
         for side, by in BOTH:
             rs_send_one(k, h, p, 4 + side, part.at[far + (cols_of(h, p, side),)],
                         t1.at[k, m, side], near(h, 1, by))
@@ -342,6 +347,9 @@
             rs[k, m, 7].wait_recv()
             value = part[(k, z, x, slice(None), cols_of(m // 2, m % 2))].astype(F32)
             value += t2[k, m, 0].astype(F32) + t2[k, m, 1].astype(F32)
+            if k == CHUNKS - 1:
+                rs[k, m, 4].wait_recv()
+                value += t3[m].astype(F32)
             for q in range(2):
                 at = (2 * m + q) * BLOCK
                 fin[at:at + BLOCK, :eighth] = value[:, q * eighth:(q + 1) * eighth].astype(BF16)
@@ -412,6 +420,9 @@
     g2(0,0,1)
     g2(0,1,0)
     g2(0,1,1)
+    assemble(1)
+    g1(1)
+    disperse(2)
     g4(0,1,0,0)
     g4(0,1,0,1)
     g4(0,0,0,0)
@@ -421,24 +432,23 @@
     g4(0,0,1,1)
     g4(0,1,1,0)
     g4(0,1,1,1)
-    assemble(1)
-    g1(1)
-    disperse(2)
     g4(0,0,2,0)
     g4(0,0,2,1)
     g4(0,1,2,0)
     g4(0,1,2,1)
     g3(0,1)
+    g2(1,0,0)
+    g2(1,0,1)
+    g2(1,1,0)
+    g2(1,1,1)
+    assemble(2)
+    g1(2)
+    g4(1,1,0,0)
+    g4(1,1,0,1)
+    g4(1,0,0,0)
+    g4(1,0,0,1)
     g4(0,0,3,0)
     g4(0,0,3,1)
-    g2(1,0,0)
-    g2(1,0,1)
-    g4(1,1,0,0)
-    g4(1,1,0,1)
-    g2(1,1,0)
-    g2(1,1,1)
-    g4(1,0,0,0)
-    g4(1,0,0,1)
     g4(0,1,3,0)
     g4(0,1,3,1)
     g3(1,0)
@@ -446,40 +456,38 @@
     g4(1,0,1,1)
     g4(1,1,1,0)
     g4(1,1,1,1)
-    assemble(2)
-    g1(2)
     g4(1,0,2,0)
     g4(1,0,2,1)
     g4(1,1,2,0)
     g4(1,1,2,1)
     g3(1,1)
+    g2(2,0,0)
+    g2(2,0,1)
+    g2(2,1,0)
+    g2(2,1,1)
+    g4(2,1,0,0)
+    g4(2,1,0,1)
+    g4(2,0,0,0)
+    g4(2,0,0,1)
     g5(0)
     for copy in loads:
         copy.wait()
     products(0,0,3)
     g4(1,0,3,0)
+    g4(1,0,3,1)
     products(0,3,4)
-    g4(1,0,3,1)
-    g2(2,0,0)
-    g2(2,0,1)
     forward(0)
+    g4(1,1,3,0)
+    g4(1,1,3,1)
     backward(0,0,0)
     backward(0,0,1)
     backward(0,1,0)
-    g4(2,1,0,0)
+    g3(2,0)
     backward(0,1,1)
-    g2(2,1,0)
-    g4(2,1,0,1)
-    g2(2,1,1)
-    g4(2,0,0,0)
-    g4(2,0,0,1)
-    g4(1,1,3,0)
-    g4(1,1,3,1)
-    g3(2,0)
-    g4(2,1,1,1)
     g4(2,0,1,0)
     g4(2,0,1,1)
     g4(2,1,1,0)
+    g4(2,1,1,1)
     g4(2,0,2,0)
     g4(2,0,2,1)
     g4(2,1,2,0)
@@ -490,24 +498,24 @@
     r1(0,0,1)
     r1(0,1,0)
     r1(0,1,1)
-    products(1,0,3)
+    products(1,0,2)
     g4(2,0,3,0)
-    products(1,3,4)
     g4(2,0,3,1)
+    products(1,2,4)
+    g4(2,1,3,0)
+    g4(2,1,3,1)
     forward(1)
-    g4(2,1,3,0)
     backward(1,0,0)
-    g4(2,1,3,1)
-    backward(1,0,1)
-    backward(1,1,0)
     r2(0,0,1,0)
     r2(0,0,1,1)
     r2(0,0,0,0)
-    backward(1,1,1)
+    backward(1,0,1)
     r2(0,1,1,0)
     r2(0,0,0,1)
     r2(0,1,1,1)
+    backward(1,1,0)
     r2(0,1,0,0)
+    backward(1,1,1)
     r2(0,1,0,1)
     g5(2)
     r1(1,0,0)
@@ -576,21 +584,15 @@
     weight_in(7,9)
     r3(2,0,0)
     weight_in(9,10)
-    weight_down(0,2)
-    r4(2,0,1,0)
+    weight_down(0,1)
     r3(2,1,1)
+    weight_down(1,2)
     r3(2,1,0)
-    r4(2,0,0,0)
-    r4(2,0,0,1)
     weight_down(2,4)
     r5(1)
-    r4(2,0,1,1)
-    r4(2,1,0,0)
-    r4(2,1,0,1)
-    r4(2,1,1,0)
-    r4(2,1,1,1)
-    weight_down(4,10)
+    weight_down(4,8)
     r5(2)
+    weight_down(8,10)
 
     for k in range(CHUNKS):
         for dc in range(1, OWNERS):
@@ -672,6 +674,7 @@
             pltpu.VMEM((CHUNKS, 4, 2, SIDE, BLOCK, quarter), BF16),
             pltpu.VMEM((CHUNKS, 4, 2, BLOCK, eighth), BF16),
             pltpu.VMEM((CHUNKS, 4, 2, BLOCK, quarter), BF16),
+            pltpu.VMEM((4, BLOCK, quarter), BF16),
             pltpu.VMEM((8 * BLOCK, eighth + LANES), BF16),
             pltpu.VMEM((CHUNKS, OWNERS, BLOCK, eighth + LANES), BF16),
             pltpu.VMEM((ROWS, 3 * units), F32),

time: 160 us -> 157 us (0.981)
  Pallas kernels: 158 us -> 155 us
    pallas_call x1, Pallas kernels: 153 us -> 150 us  [per_device(): pl.pallas_call(kernel, out_shape=(pltpu.VMEM((CHUNKS, OWNERS, BLOCK, eigh...]
where the time goes in v5:
time: 157 us; the launch traced here: 156 us
  Pallas kernels  155 us (99%)
    pallas_call x1, Pallas kernels, per_device(): pl.pallas_call(kernel, out_shape=(pltpu.VMEM((CHUNKS, OWNERS, BLOCK, eigh...  150 us
    pallas_call x1, Pallas kernels, per_device(): pl.pallas_call(finish, out_shape=(jax.ShapeDtypeStruct((count, width), BF...  5.19 us

profile of v5, /device:TPU:0, one launch (start us, length us, event | category | flops | bytes accessed | tf_op | source)
XLA Modules:
  0.0 155.8 jit_solution(10609537065870420617)
XLA Ops:
  0.6 0.0 copy-start
  0.6 149.7 %shard_map.110 = (bf16[3,8,16,768]{3,2,1,0:T(8,128)(2,1)S(1)}, bf16[1,5120,384]{2,1,0:T(8,128)(2,1)S(1)}, bf16[1,5120,384]{2,1,0:T(8,128)(2,1)S(1)}, bf16[1,384,5120]{2,1,0:T(8,128)(2,1)S(1)}) custom-call(bf16[32,5120]{1,0:T(8,128)(2,1)} %tokens.1, bf16[32,5120]{1,0:T(8,128)(2,1)} %grads.1, bf16[1,32]{1,0:T(2,128)(2,1)} %bitcast.5, s32[1,32]{1,0:T(1,128)} %bitcast.3, ...), custom_call_target="tpu_custom_call" | custom-call | tf_op jit(solution)/shard_map/pallas_call | solution.py:656
  150.4 0.0 copy-done
  150.4 5.2 %shard_map.111 = (bf16[32,5120]{1,0:T(8,128)(2,1)}, bf16[1,32]{1,0:T(2,128)(2,1)}, bf16[1,5120,384]{2,1,0:T(8,128)(2,1)}, bf16[1,5120,384]{2,1,0:T(8,128)(2,1)}, bf16[1,384,5120]{2,1,0:T(8,128)(2,1)}) custom-call(s32[1,32]{1,0:T(1,128)S(1)} %bitcast.4, bf16[3,8,16,768]{3,2,1,0:T(8,128)(2,1)S(1)} %get-tuple-element.14.back_in, ...), custom_call_target="tpu_custom_call" | custom-call | tf_op jit(solution)/shard_map/pallas_call | solution.py:702
Async XLA Ops:
  0.6 149.7 %copy-start = (s32[32,1]{0,1:T(1,128)S(1)}, s32[32,1]{0,1:T(1,128)}, u32[]{:S(2)}) copy-start(s32[32,1]{0,1:T(1,128)} %param.10) | copy-start | bytes 388

commit v6 on v5

--- a/solution.py
+++ b/solution.py
@@ -541,58 +541,56 @@
     r2(1,1,1,0)
     r4(0,0,1,0)
     r2(1,1,1,1)
+    r4(0,1,1,0)
+    backward(2,0,0)
+    r4(0,0,1,1)
     r4(0,1,0,0)
     r4(0,1,0,1)
-    r4(0,1,1,0)
+    r4(0,1,1,1)
     r2(1,1,0,1)
-    r4(0,0,1,1)
-    backward(2,0,0)
-    r4(0,1,1,1)
     r1(2,0,0)
     backward(2,0,1)
     r1(2,0,1)
     backward(2,1,0)
     r1(2,1,0)
     backward(2,1,1)
-    r3(1,0,1)
     r1(2,1,1)
     probs_out()
+    r3(1,0,1)
+    weight_in(0,1)
     r3(1,0,0)
-    weight_in(0,3)
-    r3(1,1,0)
+    weight_in(1,3)
     r3(1,1,1)
     weight_in(3,4)
+    r5(0)
+    r3(1,1,0)
     r2(2,0,0,0)
     r2(2,0,1,0)
+    r2(2,0,0,1)
     r2(2,0,1,1)
-    r5(0)
+    r4(1,0,1,0)
     r4(1,0,0,0)
+    r2(2,1,0,0)
     r4(1,0,0,1)
-    r4(1,0,1,0)
+    r4(1,1,1,0)
+    r2(2,1,1,0)
+    r2(2,1,1,1)
+    weight_in(4,5)
+    r4(1,0,1,1)
+    r4(1,1,1,1)
     r4(1,1,0,0)
     r4(1,1,0,1)
-    r4(1,1,1,0)
-    r2(2,0,0,1)
-    r2(2,1,0,0)
     r2(2,1,0,1)
-    r4(1,0,1,1)
-    r2(2,1,1,0)
-    r2(2,1,1,1)
-    r4(1,1,1,1)
-    weight_in(4,7)
+    weight_in(5,9)
+    r3(2,0,0)
     r3(2,0,1)
-    weight_in(7,9)
-    r3(2,0,0)
     weight_in(9,10)
-    weight_down(0,1)
+    weight_down(0,4)
     r3(2,1,1)
-    weight_down(1,2)
     r3(2,1,0)
-    weight_down(2,4)
     r5(1)
-    weight_down(4,8)
+    weight_down(4,10)
     r5(2)
-    weight_down(8,10)
 
     for k in range(CHUNKS):
         for dc in range(1, OWNERS):

time: 157 us -> 157 us (level)
  no operation moved by 1% of the time
where the time goes in v6:
time: 157 us; the launch traced here: 156 us
  Pallas kernels  155 us (99%)
    pallas_call x1, Pallas kernels, per_device(): pl.pallas_call(kernel, out_shape=(pltpu.VMEM((CHUNKS, OWNERS, BLOCK, eigh...  150 us
    pallas_call x1, Pallas kernels, per_device(): pl.pallas_call(finish, out_shape=(jax.ShapeDtypeStruct((count, width), BF...  5.19 us

profile of v6, /device:TPU:0, one launch (start us, length us, event | category | flops | bytes accessed | tf_op | source)
XLA Modules:
  0.0 155.9 jit_solution(9357022525831209148)
XLA Ops:
  0.6 0.0 copy-start
  0.6 149.9 %shard_map.110 = (bf16[3,8,16,768]{3,2,1,0:T(8,128)(2,1)S(1)}, bf16[1,5120,384]{2,1,0:T(8,128)(2,1)S(1)}, bf16[1,5120,384]{2,1,0:T(8,128)(2,1)S(1)}, bf16[1,384,5120]{2,1,0:T(8,128)(2,1)S(1)}) custom-call(bf16[32,5120]{1,0:T(8,128)(2,1)} %tokens.1, bf16[32,5120]{1,0:T(8,128)(2,1)} %grads.1, bf16[1,32]{1,0:T(2,128)(2,1)} %bitcast.5, s32[1,32]{1,0:T(1,128)} %bitcast.3, ...), custom_call_target="tpu_custom_call" | custom-call | tf_op jit(solution)/shard_map/pallas_call | solution.py:654
  150.5 0.0 copy-done
  150.5 5.2 %shard_map.111 = (bf16[32,5120]{1,0:T(8,128)(2,1)}, bf16[1,32]{1,0:T(2,128)(2,1)}, bf16[1,5120,384]{2,1,0:T(8,128)(2,1)}, bf16[1,5120,384]{2,1,0:T(8,128)(2,1)}, bf16[1,384,5120]{2,1,0:T(8,128)(2,1)}) custom-call(s32[1,32]{1,0:T(1,128)S(1)} %bitcast.4, bf16[3,8,16,768]{3,2,1,0:T(8,128)(2,1)S(1)} %get-tuple-element.14.back_in, ...), custom_call_target="tpu_custom_call" | custom-call | tf_op jit(solution)/shard_map/pallas_call | solution.py:700
Async XLA Ops:
  0.6 149.9 %copy-start = (s32[32,1]{0,1:T(1,128)S(1)}, s32[32,1]{0,1:T(1,128)}, u32[]{:S(2)}) copy-start(s32[32,1]{0,1:T(1,128)} %param.10) | copy-start | bytes 388
